TPU v7x, 32 devices: a whole 2x2x4 slice. The times are simulated.
32 devices in a mesh: seq: 2 (over x), exp: 8 (over z, y), dp: 2 (over core).
Axes of the slice: x: 2, y: 2, z: 4, core: 2. Of those that a mesh axis runs over, the one named last changes fastest.
Arguments:
- tokens: bfloat16 [2, 16, 768, 768], P(None, ('exp', 'dp'), 'seq'), may hold values from -6 to 6
- first_gain: bfloat16 [768], P('dp'), may hold values from 0.5 to 1.5
- first_shift: bfloat16 [768], P('dp'), may hold values from -1.5 to 1.5
- attention_in: bfloat16 [768, 2304], P('dp'), may hold values from -0.21875 to 0.21875
- attention_out: bfloat16 [768, 768], P('dp'), may hold values from -1.75 to 1.75
- second_gain: bfloat16 [768], P('dp'), may hold values from 0.5 to 1.5
- second_shift: bfloat16 [768], P('dp'), may hold values from -1.5 to 1.5
- router_weight: bfloat16 [768, 8], P('dp'), may hold values from -0.15625 to 0.15625
- up_weight: bfloat16 [8, 768, 3072], P('exp', 'dp'), may hold values from -0.21875 to 0.21875
- down_weight: bfloat16 [8, 3072, 768], P('exp', 'dp'), may hold values from -0.15625 to 0.15625
- routes: int32 [2, 16, 768, 2], P(None, ('exp', 'dp'), 'seq'), may hold values from 0 to 7, all different within a row
- priority: int32 [2, 16, 768], P(None, ('exp', 'dp'), 'seq'), may hold values from 0 to 1048575
- lengths: int32 [2, 16, 4], P(None, ('exp', 'dp')), may hold values from 0 to 576, as said below
- out_cotangent: bfloat16 [2, 16, 768, 768], P(None, ('exp', 'dp'), 'seq'), may hold values from -6 to 6
Outputs:
- mixed: bfloat16 [2, 16, 768, 768], P(None, ('exp', 'dp'), 'seq')
- tokens_grad: bfloat16 [2, 16, 768, 768], P(None, ('exp', 'dp'), 'seq')
- first_gain_grad: float32 [768], P('dp')
- first_shift_grad: float32 [768], P('dp')
- attention_in_grad: float32 [768, 2304], P('dp')
- attention_out_grad: float32 [768, 768], P('dp')
- second_gain_grad: float32 [768], P('dp')
- second_shift_grad: float32 [768], P('dp')
- router_weight_grad: float32 [768, 8], P('dp')
- up_weight_grad: float32 [8, 768, 3072], P('exp', 'dp')
- down_weight_grad: float32 [8, 3072, 768], P('exp', 'dp')
Inputs may be any that keep to these rules, and one draw needn't show every extreme that they name: `routes`: each patch names two different experts. Each sequence is grouped by resolution: either one image of 576 patches followed by a padding document of 192 patches and two empty entries, or three images of 196 patches followed by a padding document of 180 patches; padding rows form a document of their own; the 4 lengths of one sequence sum to 768.
All inputs are finite; a program needn't handle non-finite values.
Results may differ from a plain program's by a relative error of at most 0.015.
Values may be sent and summed in bfloat16 or wider, within the bound.
A program may use at most 256 MiB of HBM per device.

v0:
```python
from functools import partial

import jax
import jax.numpy as jnp
from jax import lax
from jax.sharding import PartitionSpec as P

HEADS = 12


EPSILON = 1e-06
HIGHEST = lax.Precision.HIGHEST


def layer_norm(values, gain, shift):
    centre = values - jnp.mean(values, axis=-1, keepdims=True)
    spread = jnp.mean(centre * centre, axis=-1, keepdims=True)
    return centre * lax.rsqrt(spread + EPSILON) * gain + shift


def doc_ids(length_row, total):
    bounds = jnp.cumsum(length_row)
    places = jnp.arange(total, dtype=jnp.int32)
    return jnp.sum((places[:, None] >= bounds[None, :]).astype(jnp.int32), axis=1)


def assign(route_block, level_block, experts, capacity):
    count = route_block.shape[0] * 2
    wanted = route_block.reshape(-1)
    places = jnp.arange(count, dtype=jnp.int32)
    order_k = places % 2
    owner = places // 2
    level = jnp.repeat(level_block, 2)
    ahead = (order_k[None, :] < order_k[:, None]) | (order_k[None, :] == order_k[:, None]) & (
        (level[None, :] > level[:, None])
        | (level[None, :] == level[:, None]) & (owner[None, :] < owner[:, None])
    )
    queue = jnp.sum((ahead & (wanted[None, :] == wanted[:, None])).astype(jnp.int32), axis=1)
    kept = queue < capacity
    slot = jnp.where(kept, wanted * capacity + queue, 0)
    cells = jnp.arange(experts * capacity, dtype=jnp.int32)
    match = (slot[None, :] == cells[:, None]) & kept[None, :]
    source = jnp.sum(jnp.where(match, owner[None, :], 0), axis=1)
    picked = jnp.sum(jnp.where(match, places[None, :], 0), axis=1)
    filled = jnp.any(match, axis=1)
    return (slot, kept, source, picked, filled)


def expert_forward(arrived, up_matrix, down_matrix):
    hidden = jnp.einsum("ecd,df->ecf", arrived, up_matrix, preferred_element_type=jnp.float32)
    active = jax.nn.gelu(hidden, approximate=False).astype(jnp.bfloat16)
    produced = jnp.einsum(
        "ecf,fd->ecd", active, down_matrix, preferred_element_type=jnp.float32
    ).astype(jnp.bfloat16)
    return (produced, arrived, hidden)


def body(
    tokens,
    first_gain,
    first_shift,
    attention_in,
    attention_out,
    second_gain,
    second_shift,
    router_weight,
    up_weight,
    down_weight,
    routes,
    priority,
    lengths,
    out_cotangent,
):
    micro_count = tokens.shape[0]
    tok_rows = tokens.shape[2]
    width = tokens.shape[3]
    head_dim = width // HEADS
    scale = head_dim ** (-0.5)
    span = lax.axis_size("seq") * tok_rows
    own_start = lax.axis_index("seq") * tok_rows
    experts = lax.axis_size("exp") * up_weight.shape[0]
    hidden_width = up_weight.shape[2]
    capacity = (210 * tok_rows + 100 * experts - 1) // (100 * experts)
    gain_one_sum = jnp.zeros((width,), jnp.float32)
    shift_one_sum = jnp.zeros((width,), jnp.float32)
    in_sum = jnp.zeros((width, 3 * width), jnp.float32)
    out_sum = jnp.zeros((width, width), jnp.float32)
    gain_two_sum = jnp.zeros((width,), jnp.float32)
    shift_two_sum = jnp.zeros((width,), jnp.float32)
    router_sum = jnp.zeros((width, experts), jnp.float32)
    up_sum = jnp.zeros((width, hidden_width), jnp.float32)
    down_sum = jnp.zeros((hidden_width, width), jnp.float32)
    mixed_parts = []
    input_grads = []
    for micro in range(micro_count):
        gathered = (
            lax.all_gather(first_gain, "dp", axis=0, tiled=True),
            lax.all_gather(first_shift, "dp", axis=0, tiled=True),
            lax.all_gather(attention_in, "dp", axis=0, tiled=True),
            lax.all_gather(attention_out, "dp", axis=0, tiled=True),
            lax.all_gather(second_gain, "dp", axis=0, tiled=True),
            lax.all_gather(second_shift, "dp", axis=0, tiled=True),
            lax.all_gather(router_weight, "dp", axis=0, tiled=True),
            lax.all_gather(up_weight, "dp", axis=1, tiled=True),
            lax.all_gather(down_weight, "dp", axis=1, tiled=True),
        )
        (
            gain_one,
            shift_one,
            in_full,
            out_full,
            gain_two,
            shift_two,
            router_full,
            up_full,
            down_full,
        ) = gathered
        inputs = tokens[micro, 0].astype(jnp.float32)
        first_norm, first_pull = jax.vjp(
            layer_norm, inputs, gain_one.astype(jnp.float32), shift_one.astype(jnp.float32)
        )
        first_low = first_norm.astype(jnp.bfloat16)
        packed = jnp.dot(first_low, in_full, preferred_element_type=jnp.float32).astype(
            jnp.bfloat16
        )
        query = packed[:, :width].reshape(tok_rows, HEADS, head_dim)
        pairs = lax.all_gather(packed[:, width:], "seq", axis=0, tiled=True)
        keys = pairs[:, :width].reshape(span, HEADS, head_dim)
        values = pairs[:, width:].reshape(span, HEADS, head_dim)
        documents = doc_ids(lengths[micro, 0], span)
        own_docs = lax.dynamic_slice_in_dim(documents, own_start, tok_rows)
        visible = (own_docs[:, None] == documents[None, :])[None]

        def score_rows():
            raw = (
                jnp.einsum("qhd,khd->hqk", query, keys, preferred_element_type=jnp.float32) * scale
            )
            return jnp.where(visible, raw, -1e30)

        scores = score_rows()
        peak = jnp.max(scores, axis=-1, keepdims=True)
        raised = jnp.exp(scores - peak)
        total = jnp.sum(raised, axis=-1, keepdims=True)
        weighting = raised / total
        log_total = peak + jnp.log(total)
        attended = (
            jnp.einsum(
                "hqk,khd->qhd",
                weighting.astype(jnp.bfloat16),
                values,
                preferred_element_type=jnp.float32,
            )
            .reshape(tok_rows, width)
            .astype(jnp.bfloat16)
        )
        residual = inputs + jnp.dot(attended, out_full, preferred_element_type=jnp.float32)
        second_norm, second_pull = jax.vjp(
            layer_norm, residual, gain_two.astype(jnp.float32), shift_two.astype(jnp.float32)
        )
        moe_input = second_norm.astype(jnp.bfloat16)
        logits = jnp.dot(moe_input, router_full, preferred_element_type=jnp.float32)
        picks = (routes[micro, 0][:, :, None] == jnp.arange(experts, dtype=jnp.int32)).astype(
            jnp.float32
        )

        def gating(logit_rows):
            return jax.nn.softmax(jnp.sum(picks * logit_rows[:, None, :], axis=-1), axis=-1)

        gate, gate_pull = jax.vjp(gating, logits)
        slot, kept, source, picked, filled = assign(
            routes[micro, 0], priority[micro, 0], experts, capacity
        )
        outgoing = jnp.where(filled[:, None], jnp.take(moe_input, source, axis=0), 0.0).reshape(
            experts, capacity, width
        )
        produced, arrived, hidden = expert_forward(
            lax.all_to_all(outgoing, "exp", split_axis=0, concat_axis=0, tiled=True),
            up_full[0],
            down_full[0],
        )
        returned = lax.all_to_all(produced, "exp", split_axis=0, concat_axis=0, tiled=True).reshape(
            experts * capacity, width
        )
        chosen_rows = jnp.where(
            kept[:, None], jnp.take(returned, slot, axis=0).astype(jnp.float32), 0.0
        ).reshape(tok_rows, 2, width)
        mixed_parts.append(
            (residual + jnp.sum(gate[:, :, None] * chosen_rows, axis=1)).astype(jnp.bfloat16)
        )
        upstream = out_cotangent[micro, 0].astype(jnp.float32)
        row_grads = upstream[:, None, :] * gate[:, :, None]
        gate_grad = jnp.sum(upstream[:, None, :] * chosen_rows, axis=-1)
        back_rows = (
            jnp.where(
                filled[:, None],
                jnp.take(row_grads.reshape(2 * tok_rows, width), picked, axis=0),
                0.0,
            )
            .astype(jnp.bfloat16)
            .reshape(experts, capacity, width)
        )
        at_expert = lax.all_to_all(back_rows, "exp", split_axis=0, concat_axis=0, tiled=True)
        active, gelu_pull = jax.vjp(partial(jax.nn.gelu, approximate=False), hidden)
        down_sum = down_sum + jnp.einsum(
            "ecf,ecd->fd",
            active.astype(jnp.bfloat16),
            at_expert,
            preferred_element_type=jnp.float32,
        )
        active_grad = jnp.einsum(
            "ecd,fd->ecf", at_expert, down_full[0], preferred_element_type=jnp.float32
        )
        hidden_grad = gelu_pull(active_grad)[0].astype(jnp.bfloat16)
        up_sum = up_sum + jnp.einsum(
            "ecd,ecf->df", arrived, hidden_grad, preferred_element_type=jnp.float32
        )
        arrived_grad = jnp.einsum(
            "ecf,df->ecd", hidden_grad, up_full[0], preferred_element_type=jnp.float32
        ).astype(jnp.bfloat16)
        source_grad = lax.all_to_all(
            arrived_grad, "exp", split_axis=0, concat_axis=0, tiled=True
        ).reshape(experts * capacity, width)
        moe_grad = jnp.sum(
            jnp.where(
                kept[:, None], jnp.take(source_grad, slot, axis=0).astype(jnp.float32), 0.0
            ).reshape(tok_rows, 2, width),
            axis=1,
        )
        logit_grad = gate_pull(gate_grad)[0]
        moe_grad = moe_grad + jnp.dot(
            logit_grad, router_full.astype(jnp.float32).T, precision=HIGHEST
        )
        router_sum = router_sum + jnp.dot(
            moe_input.astype(jnp.float32).T, logit_grad, precision=HIGHEST
        )
        residual_grad, gain_two_grad, shift_two_grad = second_pull(moe_grad)
        gain_two_sum = gain_two_sum + gain_two_grad
        shift_two_sum = shift_two_sum + shift_two_grad
        residual_grad = residual_grad + upstream
        branch_grad = residual_grad.astype(jnp.bfloat16)
        out_sum = out_sum + jnp.einsum(
            "td,te->de", attended, branch_grad, preferred_element_type=jnp.float32
        )
        attended_grad = (
            jnp.dot(branch_grad, out_full.T, preferred_element_type=jnp.float32)
            .astype(jnp.bfloat16)
            .reshape(tok_rows, HEADS, head_dim)
        )
        again = jnp.exp(score_rows() - log_total)
        weighting_grad = jnp.einsum(
            "qhd,khd->hqk", attended_grad, values, preferred_element_type=jnp.float32
        )
        values_grad = jnp.einsum(
            "hqk,qhd->khd",
            again.astype(jnp.bfloat16),
            attended_grad,
            preferred_element_type=jnp.float32,
        )
        inner = jnp.sum(again * weighting_grad, axis=-1, keepdims=True)
        scores_grad = (again * (weighting_grad - inner)).astype(jnp.bfloat16)
        query_grad = (
            jnp.einsum("hqk,khd->qhd", scores_grad, keys, preferred_element_type=jnp.float32)
            * scale
        )
        keys_grad = (
            jnp.einsum("hqk,qhd->khd", scores_grad, query, preferred_element_type=jnp.float32)
            * scale
        )
        pair_terms = jnp.concatenate(
            [keys_grad.reshape(span, width), values_grad.reshape(span, width)], axis=1
        )
        pair_grad = lax.psum_scatter(
            pair_terms.astype(jnp.bfloat16), "seq", scatter_dimension=0, tiled=True
        ).astype(jnp.float32)
        packed_grad = jnp.concatenate(
            [query_grad.reshape(tok_rows, width), pair_grad], axis=1
        ).astype(jnp.bfloat16)
        in_sum = in_sum + jnp.einsum(
            "td,te->de", first_low, packed_grad, preferred_element_type=jnp.float32
        )
        first_grad = jnp.dot(packed_grad, in_full.T, preferred_element_type=jnp.float32)
        token_grad, gain_one_grad, shift_one_grad = first_pull(first_grad)
        gain_one_sum = gain_one_sum + gain_one_grad
        shift_one_sum = shift_one_sum + shift_one_grad
        input_grads.append((token_grad + residual_grad).astype(jnp.bfloat16))
    sum_a, sum_b, sum_c, sum_d, sum_e, sum_f, sum_g = lax.psum(
        (gain_one_sum, shift_one_sum, in_sum, out_sum, gain_two_sum, shift_two_sum, router_sum),
        ("seq", "exp"),
    )
    shares = (
        lax.psum_scatter(sum_a.astype(jnp.bfloat16), "dp", scatter_dimension=0, tiled=True).astype(
            jnp.float32
        ),
        lax.psum_scatter(sum_b.astype(jnp.bfloat16), "dp", scatter_dimension=0, tiled=True).astype(
            jnp.float32
        ),
        lax.psum_scatter(sum_c.astype(jnp.bfloat16), "dp", scatter_dimension=0, tiled=True).astype(
            jnp.float32
        ),
        lax.psum_scatter(sum_d.astype(jnp.bfloat16), "dp", scatter_dimension=0, tiled=True).astype(
            jnp.float32
        ),
        lax.psum_scatter(sum_e.astype(jnp.bfloat16), "dp", scatter_dimension=0, tiled=True).astype(
            jnp.float32
        ),
        lax.psum_scatter(sum_f.astype(jnp.bfloat16), "dp", scatter_dimension=0, tiled=True).astype(
            jnp.float32
        ),
        lax.psum_scatter(sum_g.astype(jnp.bfloat16), "dp", scatter_dimension=0, tiled=True).astype(
            jnp.float32
        ),
    )
    up_split, down_split = (
        lax.psum_scatter(
            up_sum[None].astype(jnp.bfloat16), "dp", scatter_dimension=1, tiled=True
        ).astype(jnp.float32),
        lax.psum_scatter(
            down_sum[None].astype(jnp.bfloat16), "dp", scatter_dimension=1, tiled=True
        ).astype(jnp.float32),
    )
    up_total, down_total = (
        lax.psum(up_split.astype(jnp.bfloat16), "seq").astype(jnp.float32),
        lax.psum(down_split.astype(jnp.bfloat16), "seq").astype(jnp.float32),
    )
    mixed = jnp.stack(mixed_parts)[:, None]
    tokens_grad = jnp.stack(input_grads)[:, None]
    return (
        mixed,
        tokens_grad,
        shares[0],
        shares[1],
        shares[2],
        shares[3],
        shares[4],
        shares[5],
        shares[6],
        up_total,
        down_total,
    )


def solution(mesh):
    placed = (
        P(None, ("exp", "dp"), "seq", None),
        P("dp"),
        P("dp"),
        P("dp", None),
        P("dp", None),
        P("dp"),
        P("dp"),
        P("dp", None),
        P("exp", "dp", None),
        P("exp", "dp", None),
        P(None, ("exp", "dp"), "seq", None),
        P(None, ("exp", "dp"), "seq"),
        P(None, ("exp", "dp"), None),
        P(None, ("exp", "dp"), "seq", None),
    )
    return jax.shard_map(
        body,
        mesh=mesh,
        in_specs=placed,
        out_specs=(
            P(None, ("exp", "dp"), "seq", None),
            P(None, ("exp", "dp"), "seq", None),
            P("dp"),
            P("dp"),
            P("dp", None),
            P("dp", None),
            P("dp"),
            P("dp"),
            P("dp", None),
            P("exp", "dp", None),
            P("exp", "dp", None),
        ),
        check_vma=False,
    )
```

profile of v0, /device:TPU:0, one launch (start us, length us, event | category | flops | bytes accessed | tf_op | source)
XLA Modules:
  0.0 1203.3 jit_solution(17606080557780628619)
XLA Ops:
  14.5 10.5 all-gather.11.cloned.1.call-done
  59.2 8.0 all-gather.21.cloned.1.call-done
  88.9 28.3 %all-gather.13.cloned.1.call-done = bf16[768,1536]{1,0:T(8,128)(2,1)} async-done(((bf16[384,1536]{1,0:T(8,128)(2,1)}), bf16[768,1536]{1,0:T(8,128)(2,1)}) %all-gather.13.cloned.1.call-update) | async-done | bytes 2359312 | tf_op jit(solution)/shard_map/all_gather | solution.py:127
  148.1 5.7 all-to-all-start
  188.6 8.9 fusion.44
  201.2 23.8 %multiply_convert_fusion.3 = (bf16[8,101,3072]{2,1,0:T(8,128)(2,1)}, f32[8,101,3072]{2,1,0:T(8,128)}) fusion(f32[8,101,3072]{2,1,0:T(8,128)S(1)} %get-tuple-element.160, u8[101,3072]{1,0:T(8,128)(4,1)S(1)} %get-tuple-element.59, u8[101,3072]{1,0:T(8,128)(4,1)S(1)} %get-tuple-element.58), kind=kLoop, calls=%fused_computation.52 | loop fusion | flops 173752320 | bytes 25442304 | tf_op jit(solution)/shard_map/convert_element_type | solution.py:51
  225.1 9.1 fusion.62
  234.1 6.3 all-to-all-start.1
  240.5 8.6 fusion.45
  249.0 23.8 %multiply_convert_fusion.2 = (bf16[8,101,3072]{2,1,0:T(8,128)(2,1)S(1)}, f32[8,101,3072]{2,1,0:T(8,128)}) fusion(f32[8,101,3072]{2,1,0:T(8,128)S(1)} %get-tuple-element.159, u8[101,3072]{1,0:T(8,128)(4,1)S(1)} %get-tuple-element.61, u8[101,3072]{1,0:T(8,128)(4,1)S(1)} %get-tuple-element.60), kind=kLoop, calls=%fused_computation.39 | loop fusion | flops 173752320 | bytes 25442304 | tf_op jit(solution)/shard_map/convert_element_type | solution.py:51
  275.1 7.7 fusion.65
  282.8 6.5 all-to-all-start.3
  312.7 6.7 all-to-all-done.3
  345.1 8.8 all-to-all-done.4
  357.6 13.3 %add_convert_fusion.1 = bf16[8,101,3072]{2,1,0:T(8,128)(2,1)S(1)} fusion(f32[8,101,3072]{2,1,0:T(8,128)} %get-tuple-element.110, f32[8,101,3072]{2,1,0:T(8,128)} %copy-done.25, bf16[8,101,768]{2,1,0:T(8,128)(2,1)} %all-to-all-done.4, bf16[1,3072,768]{2,1,0:T(8,128)(2,1)} %all-gather.19.cloned.1.call-done), kind=kOutput, calls=%fused_computation.38 | convolution fusion | flops 3847372800 | bytes 30781440 | tf_op jit(solution)/shard_map/ecd,fd->ecf/dot_general | solution.py:210
  378.5 9.8 all-to-all-done.6
  391.9 11.7 add_convert_fusion
  405.8 7.6 fusion.59
  413.4 9.4 all-to-all-done.5
  483.8 9.0 fusion.71
  492.9 10.4 multiply_reduce_fusion
  503.3 6.9 multiply_convert_fusion
  521.7 14.2 %multiply_reduce_fusion.1 = (f32[12,384]{1,0:T(8,128)S(1)}, f32[12,384,768]{2,1,0:T(8,128)}) fusion(f32[12,384,768]{2,1,0:T(8,128)} %copy-done, f32[12,384]{1,0:T(8,128)} %log_add_fusion.1, bf16[384,12,64]{0,2,1:T(8,128)(2,1)S(1)} %bitcast.296, bf16[768,12,64]{0,2,1:T(8,128)(2,1)} %bitcast.300), kind=kOutput, calls=%fused_computation.14 | convolution fusion | flops 463597056 | bytes 30117888 | tf_op jit(solution)/shard_map/qhd,khd->hqk/dot_general | solution.py:250
  535.9 6.9 multiply_convert_fusion.1
  556.1 7.9 fusion.150
  564.0 9.5 fusion.40
  573.5 7.7 fusion.151
  581.2 9.6 fusion.41
  599.9 7.5 fusion.91
  634.4 395.2 %all-reduce.11 = (bf16[768]{0:T(1024)(128)(2,1)}, bf16[768]{0:T(1024)(128)(2,1)}, bf16[768,2304]{1,0:T(8,128)(2,1)}, bf16[768,768]{1,0:T(8,128)(2,1)}, bf16[768]...) all-reduce(f32[768]{0:T(1024)} %add.274, ...), channel_id=1, replica_groups=mesh['seq'=2,'exp'=8,'dp'=2] {'seq','exp'}, use_global_device_ids=true, to_apply=%region_54.58 | all-reduce | flops 2368512 | bytes 14211072 | tf_op jit(solution)/shard_map/psum | solution.py:286
  1055.0 11.3 reduce-scatter.14.cloned.1.call-done
  1069.9 119.6 %all-reduce.10.cloned.1.call-done = (bf16[1,384,3072]{2,1,0:T(8,128)(2,1)}, bf16[1,1536,768]{2,1,0:T(8,128)(2,1)}) async-done(((bf16[1,384,3072]{2,1,0:T(8,128)(2,1)}, bf16[1,1536,768]{2,1,0:T(8,128)(2,1)}), (bf16[1,384,3072]{2,1,0:T(8,128)(2,1)}, bf16[1,1536,768]{2,1,0:T(8,128)(2,1)})) %all-reduce.10.cloned.1.call-update) | async-done | bytes 4718608 | tf_op jit(solution)/shard_map/psum | solution.py:322
  (613 shorter events, 356.1 us)
Async XLA Ops:
  7.2 17.8 %all-gather.11.cloned.1.call-start = ((), (), s32[]{:S(2)}) async-start(), calls=%async_computation.15 | async-start | bytes 5308416 | tf_op jit(solution)/shard_map/all_gather | solution.py:99
  7.9 59.3 %all-gather.21.cloned.1.call-start = ((), (), s32[]{:S(2)}) async-start(), calls=%async_computation.20 | async-start | bytes 3538944 | tf_op jit(solution)/shard_map/all_gather | solution.py:127
  29.8 55.8 %all-gather.15.cloned.1.call-start = ((), (), s32[]{:S(2)}) async-start(), calls=%async_computation.17 | async-start | bytes 1769472 | tf_op jit(solution)/shard_map/all_gather | solution.py:100
  30.6 86.7 %all-gather.13.cloned.1.call-start = ((), (), s32[]{:S(2)}) async-start(), calls=%async_computation.16 | async-start | bytes 3538944 | tf_op jit(solution)/shard_map/all_gather | solution.py:127
  36.7 151.8 %all-gather.17.cloned.1.call-start = ((), (), s32[]{:S(2)}) async-start(), calls=%async_computation.18 | async-start | bytes 7077888 | tf_op jit(solution)/shard_map/all_gather | solution.py:104
  37.4 187.7 %all-gather.19.cloned.1.call-start = ((), (), s32[]{:S(2)}) async-start(), calls=%async_computation.19 | async-start | bytes 7077888 | tf_op jit(solution)/shard_map/all_gather | solution.py:105
  51.9 87.4 %copy-start.86 = (f32[768]{0:T(1024)}, f32[768]{0:T(1024)S(1)}, u32[]{:S(2)}) copy-start(f32[768]{0:T(1024)S(1)} %reshape.715) | copy-start | bytes 9220
  87.9 51.4 %copy-start.12 = (f32[384,768]{1,0:T(8,128)}, f32[384,768]{1,0:T(8,128)S(1)}, u32[]{:S(2)}) copy-start(f32[384,768]{1,0:T(8,128)S(1)} %get-tuple-element.158) | copy-start | bytes 3538948
  88.0 51.4 %copy-start.88 = (f32[384]{0:T(512)}, f32[384]{0:T(512)S(1)}, u32[]{:S(2)}) copy-start(f32[384]{0:T(512)S(1)} %broadcast_multiply_fusion.2) | copy-start | bytes 4612
  88.9 50.4 %copy-start.102 = (f32[384]{0:T(512)}, f32[384]{0:T(512)S(1)}, u32[]{:S(2)}) copy-start(f32[384]{0:T(512)S(1)} %fusion.124) | copy-start | bytes 4612
  140.1 149.3 %copy-start.4 = (bf16[384,768]{1,0:T(8,128)(2,1)}, bf16[384,768]{1,0:T(8,128)(2,1)S(1)}, u32[]{:S(2)}) copy-start(bf16[384,768]{1,0:T(8,128)(2,1)S(1)} %get-tuple-element.129) | copy-start | bytes 1769476
  140.1 149.6 %copy-start.2 = (bf16[384,768]{1,0:T(8,128)(2,1)}, bf16[384,768]{1,0:T(8,128)(2,1)S(1)}, u32[]{:S(2)}) copy-start(bf16[384,768]{1,0:T(8,128)(2,1)S(1)} %get-tuple-element.130) | copy-start | bytes 1769476
  148.1 36.5 %all-to-all-start = ((bf16[8,101,768]{2,1,0:T(8,128)(2,1)}), bf16[8,101,768]{2,1,0:T(8,128)(2,1)}, u32[]{:S(2)}, u32[]{:S(2)}) async-start(bf16[8,101,768]{2,1,0:T(8,128)(2,1)} %reshape.606), calls=%async_computation | async-start | bytes 2555904 | tf_op jit(solution)/shard_map/all_to_all | solution.py:177
  165.9 127.6 %copy-start.96 = (s32[1024]{0:T(1024)}, s32[1024]{0:T(1024)S(1)}, u32[]{:S(2)}) copy-start(s32[1024]{0:T(1024)S(1)} %pad_clamp_fusion.4) | copy-start | bytes 12292
  184.6 49.5 %all-to-all-start.2 = ((bf16[8,101,768]{2,1,0:T(8,128)(2,1)}), bf16[8,101,768]{2,1,0:T(8,128)(2,1)S(1)}, u32[]{:S(2)}, u32[]{:S(2)}) async-start(bf16[8,101,768]{2,1,0:T(8,128)(2,1)} %reshape.614), calls=%async_computation.2 | async-start | bytes 2555904 | tf_op jit(solution)/shard_map/all_to_all | solution.py:177
  234.1 48.6 %all-to-all-start.1 = ((bf16[8,101,768]{2,1,0:T(8,128)(2,1)}), bf16[8,101,768]{2,1,0:T(8,128)(2,1)}, u32[]{:S(2)}, u32[]{:S(2)}) async-start(bf16[8,101,768]{2,1,0:T(8,128)(2,1)} %fusion.62), calls=%async_computation.1 | async-start | bytes 2555904 | tf_op jit(solution)/shard_map/all_to_all | solution.py:181
  249.0 23.8 %copy-start.26 = (f32[8,101,3072]{2,1,0:T(8,128)}, f32[8,101,3072]{2,1,0:T(8,128)S(1)}, u32[]{:S(2)}) copy-start(f32[8,101,3072]{2,1,0:T(8,128)S(1)} %get-tuple-element.159) | copy-start | bytes 29786116
  282.8 36.5 %all-to-all-start.3 = ((bf16[8,101,768]{2,1,0:T(8,128)(2,1)}), bf16[8,101,768]{2,1,0:T(8,128)(2,1)}, u32[]{:S(2)}, u32[]{:S(2)}) async-start(bf16[8,101,768]{2,1,0:T(8,128)(2,1)} %fusion.65), calls=%async_computation.3 | async-start | bytes 2555904 | tf_op jit(solution)/shard_map/all_to_all | solution.py:181
  319.3 34.5 %all-to-all-start.4 = ((bf16[8,101,768]{2,1,0:T(8,128)(2,1)}), bf16[8,101,768]{2,1,0:T(8,128)(2,1)}, u32[]{:S(2)}, u32[]{:S(2)}) async-start(bf16[8,101,768]{2,1,0:T(8,128)(2,1)} %reshape.617), calls=%async_computation.4 | async-start | bytes 2555904 | tf_op jit(solution)/shard_map/all_to_all | solution.py:202
  342.2 31.0 %slice-start.10 = ((s8[4718592]{0:T(1024)(128)(4,1)}), s8[524288]{0:T(1024)(128)(4,1)S(1)}, s32[]{:S(2)}) async-start(s8[4718592]{0:T(1024)(128)(4,1)} %bitcast.316), calls=%async_computation.39 | async-start | bytes 1048576
  353.8 34.4 %all-to-all-start.6 = ((bf16[8,101,768]{2,1,0:T(8,128)(2,1)}), bf16[8,101,768]{2,1,0:T(8,128)(2,1)S(1)}, u32[]{:S(2)}, u32[]{:S(2)}) async-start(bf16[8,101,768]{2,1,0:T(8,128)(2,1)} %reshape.624), calls=%async_computation.6 | async-start | bytes 2555904 | tf_op jit(solution)/shard_map/all_to_all | solution.py:202
  388.3 34.5 %all-to-all-start.5 = ((bf16[8,101,768]{2,1,0:T(8,128)(2,1)}), bf16[8,101,768]{2,1,0:T(8,128)(2,1)S(1)}, u32[]{:S(2)}, u32[]{:S(2)}) async-start(bf16[8,101,768]{2,1,0:T(8,128)(2,1)} %fusion.56), calls=%async_computation.5 | async-start | bytes 2555904 | tf_op jit(solution)/shard_map/all_to_all | solution.py:220
  422.8 34.6 %all-to-all-start.7 = ((bf16[8,101,768]{2,1,0:T(8,128)(2,1)}), bf16[8,101,768]{2,1,0:T(8,128)(2,1)}, u32[]{:S(2)}, u32[]{:S(2)}) async-start(bf16[8,101,768]{2,1,0:T(8,128)(2,1)} %fusion.59), calls=%async_computation.7 | async-start | bytes 2555904 | tf_op jit(solution)/shard_map/all_to_all | solution.py:220
  427.1 183.3 %reduce-scatter.24.cloned.1.call-start = ((), (), s32[]{:S(2)}) async-start(), calls=%async_computation.26 | async-start | bytes 3538944
  515.7 97.2 %reduce-scatter.22.cloned.1.call-start = ((), (), s32[]{:S(2)}) async-start(), calls=%async_computation.25 | async-start | bytes 3538944
  515.8 78.1 %copy-start.116 = (f32[384]{0:T(512)}, f32[384]{0:T(512)S(1)}, u32[]{:S(2)}) copy-start(f32[384]{0:T(512)S(1)} %negate_multiply_fusion.5) | copy-start | bytes 4612
  556.0 476.5 %reduce-scatter.18.cloned.1.call-start = ((), (), s32[]{:S(2)}) async-start(), calls=%async_computation.23 | async-start | bytes 7077888 | tf_op jit(solution)/shard_map/reduce_scatter | solution.py:314
  573.5 459.1 %reduce-scatter.20.cloned.1.call-start = ((), (), s32[]{:S(2)}) async-start(), calls=%async_computation.24 | async-start | bytes 7077888 | tf_op jit(solution)/shard_map/reduce_scatter | solution.py:317
  590.9 460.4 %reduce-scatter.26.cloned.1.call-start = ((), (), s32[]{:S(2)}) async-start(), calls=%async_computation.27 | async-start | bytes 294912
  1031.2 21.7 %reduce-scatter.16.cloned.1.call-start = ((), (), s32[]{:S(2)}) async-start(), calls=%async_computation.22 | async-start | bytes 1769472 | tf_op jit(solution)/shard_map/reduce_scatter | solution.py:300
  1031.7 34.6 %reduce-scatter.14.cloned.1.call-start = ((), (), s32[]{:S(2)}) async-start(), calls=%async_computation.21 | async-start | bytes 5308416 | tf_op jit(solution)/shard_map/reduce_scatter | solution.py:297
  1032.5 157.0 %all-reduce.10.cloned.1.call-start = ((), (), s32[]{:S(2)}) async-start(), calls=%async_computation.28 | async-start | bytes 9437184 | tf_op jit(solution)/shard_map/psum | solution.py:322
  (164 other events, 952.6 us)
Sparse Core Ops, SparseCore 0:
  9.6 15.3 all-gather.10
  30.0 37.2 all-gather.20
  68.8 9.2 all-gather.14
  80.0 37.2 all-gather.12
  118.7 14.4 all-gather.16
  134.5 15.6 all-gather.18
  515.8 33.0 reduce-scatter.23
  556.2 33.8 reduce-scatter.21
  592.9 12.6 reduce-scatter.17
  608.4 13.7 reduce-scatter.19
  1031.3 7.0 reduce-scatter.25
  1041.0 9.8 reduce-scatter.15
  1053.8 12.5 reduce-scatter.13
  1068.7 120.7 all-reduce.9
where the time goes:
time: 1210 us; the launch traced here: 1200 us
  blocking collectives  408 us (34%)
  waiting for transfers between devices  227 us (19%)
  matrix products  212 us (18%)
  other arithmetic  166 us (14%)
  local copies, waits for them, and re-layouts  135 us (11%)
  starting transfers between devices  38.8 us (3%)
  between operations  17.1 us (1%)
    psum x1, blocking collectives, body(): lax.psum((gain_one_sum, shift_one_sum, in_sum, out_sum, gain_two_sum, shi...  395 us
    psum x1, waiting for transfers between devices, body(): lax.psum(up_split.astype(jnp.bfloat16), 'seq').astype(jnp.float32)  120 us
    convert_element_type x2, other arithmetic, expert_forward(): active = jax.nn.gelu(hidden, approximate=False).astype(jnp.bfloat16)  47.6 us
    unnamed x359, local copies, waits for them, and re-layouts  46.3 us
    all_gather x2, waiting for transfers between devices, body(): pairs = lax.all_gather(packed[:, width:], 'seq', axis=0, tiled=True)  36.3 us
    dot_general x2, matrix products, body(): jnp.einsum('ecd,fd->ecf', at_expert, down_full[0], preferred_element_type...  25 us
    dot_general x2, matrix products, body(): jnp.einsum('qhd,khd->hqk', attended_grad, values, preferred_element_type=...  24.6 us
  transfers between devices with their start and end apart: 22, of which 11 were waited for; matrix products, arithmetic and copies ran while one was open for 34% of the time, Pallas kernels for 0%

commit v1 on v0

v1 whole, which is shorter than its diff:
```python
from functools import partial

import jax
import jax.numpy as jnp
from jax import lax
from jax.experimental import pallas as pl
from jax.experimental.pallas import tpu as pltpu
from jax.sharding import PartitionSpec as P

HEADS = 12
EPSILON = 1e-06
F32 = jnp.float32
BF16 = jnp.bfloat16
VMEM = pl.BlockSpec(memory_space=pltpu.VMEM)
SMEM = pl.BlockSpec(memory_space=pltpu.SMEM)
ROUTER_ROW = 8


def mm(a, b):
    return lax.dot_general(a, b, (((1,), (0,)), ((), ())), preferred_element_type=F32)


def mm_nt(a, b):
    return lax.dot_general(a, b, (((1,), (1,)), ((), ())), preferred_element_type=F32)


def mm_tn(a, b):
    return lax.dot_general(a, b, (((0,), (0,)), ((), ())), preferred_element_type=F32)


def iota(shape, dim):
    return lax.broadcasted_iota(jnp.int32, shape, dim)


def row_of(column, size):
    return jnp.sum(jnp.where(iota((size, size), 0) == iota((size, size), 1), column, 0.0), axis=0, keepdims=True)


def column_of(row, size):
    return jnp.sum(jnp.where(iota((size, size), 0) == iota((size, size), 1), row, 0.0), axis=1, keepdims=True)


def normalise(values):
    centre = values - jnp.mean(values, axis=-1, keepdims=True)
    spread = jnp.mean(centre * centre, axis=-1, keepdims=True)
    scale = lax.rsqrt(spread + EPSILON)
    return centre * scale, scale


def norm_backward(grad, gain, xhat, scale):
    scaled = grad * gain
    along = jnp.mean(scaled * xhat, axis=-1, keepdims=True)
    return scale * (scaled - jnp.mean(scaled, axis=-1, keepdims=True) - xhat * along)


def assign_stage(routes, level, capacity, padded):
    rows = routes.shape[0]
    level_row = level.astype(F32)
    level_column = column_of(level_row, rows)
    me, other = iota((rows, rows), 0), iota((rows, rows), 1)
    ahead = (level_row > level_column) | ((level_row == level_column) & (other < me))
    lane = iota((rows, 128), 1)
    first, second = routes[:, 0:1], routes[:, 1:2]
    wants = jnp.where((lane == first) | (lane == second + 64), 1.0, 0.0)
    count = mm(jnp.where(ahead, 1.0, 0.0).astype(BF16), wants.astype(BF16))
    total = jnp.sum(wants, axis=0, keepdims=True)
    rank_one = jnp.sum(jnp.where(lane == first, count, 0.0), axis=1, keepdims=True)
    rank_two = jnp.sum(
        jnp.where(lane == second + 64, count, 0.0) + jnp.where(lane == second, total, 0.0),
        axis=1,
        keepdims=True,
    )
    slot_one = jnp.where(rank_one < capacity, first.astype(F32) * padded + rank_one, -1.0)
    slot_two = jnp.where(rank_two < capacity, second.astype(F32) * padded + rank_two, -1.0)
    return slot_one, slot_two


def batch_of(experts, padded):
    best = 1
    for count in range(1, experts + 1):
        if experts % count == 0 and count * padded <= 256 and (count * padded) % 16 == 0:
            best = count
    return best


def spread_stage(values, slot_one, slot_two, experts, padded, store, extra=None):
    rows, width = values.shape
    one, two = row_of(slot_one, rows).astype(jnp.int32), row_of(slot_two, rows).astype(jnp.int32)
    batch = batch_of(experts, padded)
    place = iota((batch * padded, rows), 0)
    for start in range(0, experts, batch):
        here = place + start * padded
        pick = jnp.where((here == one) | (here == two), 1.0, 0.0).astype(BF16)
        block = mm(pick, values).reshape(batch, padded, width)
        if extra is not None:
            parts = []
            for inner in range(batch):
                parts.append(extra(start + inner, block[inner]))
            block = jnp.stack(parts)
        store(start, batch, block.astype(BF16))


def with_rows(block, first_row, rows):
    place = iota(block.shape, 0)
    for step, row in enumerate(rows):
        wide = jnp.concatenate([row, jnp.zeros((1, block.shape[1] - row.shape[1]), F32)], axis=1)
        block = jnp.where(place == first_row + step, wide, block)
    return block


def pieces(value, count):
    parts = []
    for _ in range(count):
        part = value.astype(BF16).astype(F32)
        parts.append(part)
        value = value - part
    return parts


def dispatch_kernel(capacity, padded, routes_ref, level_ref, cot_ref, slots_ref, sent_ref):
    slot_one, slot_two = assign_stage(routes_ref[...], level_ref[...], capacity, padded)
    lane = iota(slots_ref.shape, 1)
    slots_ref[...] = jnp.where(lane == 0, slot_one, slot_two).astype(jnp.int32)

    def store(start, batch, block):
        sent_ref[start : start + batch] = block

    spread_stage(cot_ref[...], slot_one, slot_two, sent_ref.shape[0], padded, store)


def first_kernel(tokens_ref, pack_ref, weight_ref, query_ref, pairs_ref):
    width = tokens_ref.shape[1]
    pack = pack_ref[...].astype(F32)
    xhat, _ = normalise(tokens_ref[...].astype(F32))
    low = (xhat * pack[0:1] + pack[1:2]).astype(BF16)
    query_ref[...] = mm(low, weight_ref[:, 0:width]).astype(BF16)
    for part in range(2):
        pairs_ref[:, part * width : (part + 1) * width] = mm(
            low, weight_ref[:, (part + 1) * width : (part + 2) * width]
        ).astype(BF16)


def bias_stage(lengths_ref, rows, store):
    own_start = lax.axis_index("seq") * rows
    span = lax.axis_size("seq") * rows
    ends = []
    total = 0
    for step in range(lengths_ref.shape[0]):
        total = total + lengths_ref[step]
        ends.append(total)

    def documents(place):
        found = jnp.zeros(place.shape, jnp.int32)
        for end in ends:
            found = found + jnp.where(place >= end, 1, 0)
        return found

    asked = documents(iota((1, rows), 1) + own_start)
    for half in range(2):
        start = own_start if half == 0 else span - rows - own_start
        held = documents(iota((rows, 1), 0) + start)
        store(half, jnp.where(held == asked, 0.0, -1e30))


def attend_stage(query_ref, pair_refs, bias_ref, attended_ref, stats_ref):
    rows, width = query_ref.shape
    head_dim = width // HEADS
    couple = 2 * head_dim
    low_lane = iota((1, couple), 1) < head_dim

    def step(index, _):
        lanes = pl.ds(pl.multiple_of(index * couple, couple), couple)
        value_lanes = pl.ds(pl.multiple_of(width + index * couple, couple), couple)
        query = query_ref[:, lanes].astype(F32) * head_dim**-0.5
        keys = [ref[:, lanes] for ref in pair_refs]
        values = [ref[:, value_lanes].astype(F32).T.astype(BF16) for ref in pair_refs]
        outs = []
        for head in range(2):
            mine = jnp.where(low_lane == (head == 0), query, 0.0).astype(BF16)
            scores = [mm_nt(keys[half], mine) + bias_ref[half] for half in range(2)]
            peak = jnp.maximum(*[jnp.max(part, axis=0, keepdims=True) for part in scores])
            raised = [jnp.exp(part - peak) for part in scores]
            total = sum(jnp.sum(part, axis=0, keepdims=True) for part in raised)
            here = slice(head * head_dim, (head + 1) * head_dim)
            summed = sum(mm(values[half][here], raised[half].astype(BF16)) for half in range(2))
            outs.append(summed / total)
            stats_ref[pl.ds(index * 2 + head, 1), :] = peak + jnp.log(total)
        attended_ref[:, lanes] = jnp.concatenate(outs, axis=0).T.astype(BF16)
        return 0

    lax.fori_loop(0, HEADS // 2, step, 0)


def gates_of(logits, routes):
    lane = iota(logits.shape, 1)
    chosen = [
        jnp.sum(jnp.where(lane == routes[:, k : k + 1] + ROUTER_ROW, logits, 0.0), axis=1, keepdims=True)
        for k in range(2)
    ]
    peak = jnp.maximum(*chosen)
    raised = [jnp.exp(part - peak) for part in chosen]
    total = raised[0] + raised[1]
    return raised[0] / total, raised[1] / total


def second_kernel(
    capacity,
    padded,
    tokens_ref,
    pack_ref,
    query_ref,
    own_ref,
    other_ref,
    lengths_ref,
    out_weight_ref,
    routes_ref,
    slots_ref,
    residual_ref,
    moe_input_ref,
    attended_ref,
    stats_ref,
    gates_ref,
    sent_ref,
    bias_ref,
):
    rows, width = tokens_ref.shape

    def store_bias(half, block):
        bias_ref[half] = block

    bias_stage(lengths_ref, rows, store_bias)
    attend_stage(query_ref, (own_ref, other_ref), bias_ref, attended_ref, stats_ref)
    residual = tokens_ref[...].astype(F32) + mm(attended_ref[...], out_weight_ref[...])
    residual_ref[...] = residual
    pack = pack_ref[...]
    xhat, _ = normalise(residual)
    moe_input = (xhat * pack[2:3].astype(F32) + pack[3:4].astype(F32)).astype(BF16)
    moe_input_ref[...] = moe_input
    gates = gates_of(mm_nt(moe_input, pack), routes_ref[...])
    lane = iota(gates_ref.shape, 1)
    gates_ref[...] = jnp.where(lane == 0, gates[0], gates[1])
    slots = slots_ref[...]
    slot_cols = [slots[:, k : k + 1] for k in range(2)]
    place = iota((rows, 128), 1)

    def gate_rows(expert, block):
        row = jnp.sum(
            sum(
                jnp.where(slot_cols[k] - expert * padded == place, gates[k], 0.0)
                for k in range(2)
            ),
            axis=0,
            keepdims=True,
        )
        return with_rows(block, capacity, pieces(row, 2))

    def store(start, batch, block):
        sent_ref[start : start + batch] = block

    spread_stage(
        moe_input,
        slot_cols[0].astype(F32),
        slot_cols[1].astype(F32),
        sent_ref.shape[0],
        padded,
        store,
        gate_rows,
    )


def phi_terms(hidden):
    size = jnp.abs(hidden)
    bell = jnp.exp(hidden * hidden * -0.5)
    t = 1.0 / (1.0 + 0.23164188828 * size)
    tail = t * (
        0.127414796
        + t * (-0.142248368 + t * (0.7107068705 + t * (-0.7265760135 + t * 0.5307027145)))
    )
    tail = tail * bell
    return jnp.where(hidden >= 0, 1.0 - tail, tail), bell


def expert_kernel(
    capacity,
    padded,
    chunks,
    first,
    rows_ref,
    cot_ref,
    up_ref,
    down_ref,
    *refs,
):
    if first:
        back_ref, grads_ref, up_grad_ref, down_grad_ref, x, xt, g, y, dx = refs
    else:
        up_old_ref, down_old_ref, back_ref, grads_ref, up_grad_ref, down_grad_ref, x, xt, g, y, dx = refs
    experts, _, width = rows_ref.shape
    step = pl.program_id(0)
    batch = batch_of(experts, padded)
    flat = batch * padded

    @pl.when(step == 0)
    def _():
        for start in range(0, experts, batch):
            block = rows_ref[start : start + batch].astype(F32)
            cot = cot_ref[start : start + batch].astype(F32)
            x[start * padded : start * padded + flat, :] = block.reshape(flat, width).astype(BF16)
            scaled = []
            place = iota((padded, 128), 0)
            for inner in range(batch):
                gate_row = jnp.sum(
                    jnp.where(
                        (place == capacity) | (place == capacity + 1), block[inner][:, 0:128], 0.0
                    ),
                    axis=0,
                    keepdims=True,
                )
                gate = jnp.sum(
                    jnp.where(place == iota((padded, 128), 1), gate_row, 0.0), axis=1, keepdims=True
                )
                scaled.append(cot[inner] * gate)
            g[start * padded : start * padded + flat, :] = (
                jnp.stack(scaled).reshape(flat, width).astype(BF16)
            )
        xt[...] = x[...].T
        y[...] = jnp.zeros_like(y)
        dx[...] = jnp.zeros_like(dx)

    hidden = mm(x[...], up_ref[...])
    phi, bell = phi_terms(hidden)
    active = (hidden * phi).astype(BF16)
    y[...] += mm(active, down_ref[...])
    active_grad = mm_nt(g[...], down_ref[...])
    hidden_grad = (active_grad * (phi + hidden * bell * 0.3989422804)).astype(BF16)
    dx[...] += mm_nt(hidden_grad, up_ref[...])
    up_grad = mm(xt[...], hidden_grad)
    down_grad = mm_tn(active, g[...])
    if not first:
        up_grad = up_grad + up_old_ref[...]
        down_grad = down_grad + down_old_ref[...]
    up_grad_ref[...] = up_grad
    down_grad_ref[...] = down_grad

    @pl.when(step == chunks - 1)
    def _():
        for start in range(0, experts, batch):
            here = slice(start * padded, start * padded + flat)
            produced = y[here, :].reshape(batch, padded, width).astype(BF16)
            back_ref[start : start + batch] = produced
            cot = cot_ref[start : start + batch].astype(F32)
            along = jnp.sum(cot * produced.astype(F32), axis=-1, keepdims=True)
            grads = dx[here, :].reshape(batch, padded, width)
            place, lane = iota((padded, 128), 0), iota((padded, 128), 1)
            parts = []
            for inner in range(batch):
                row = jnp.sum(
                    jnp.where(place == lane, along[inner], 0.0), axis=0, keepdims=True
                )
                parts.append(with_rows(grads[inner], capacity, pieces(row, 3)))
            grads_ref[start : start + batch] = jnp.stack(parts).astype(BF16)


def gather_stage(blocks_ref, slots, weights, padded):
    experts, _, width = blocks_ref.shape
    rows = slots.shape[0]
    batch = batch_of(experts, padded)
    place = iota((rows, batch * padded), 1)
    totals = [jnp.zeros((rows, width), F32) for _ in weights]
    for start in range(0, experts, batch):
        block = (
            blocks_ref[start : start + batch].astype(F32).reshape(batch * padded, width).astype(BF16)
        )
        here = place + start * padded
        for index, chosen in enumerate(weights):
            hit = slots[:, chosen[0] : chosen[0] + 1] == here
            for k in chosen[1:]:
                hit = hit | (slots[:, k : k + 1] == here)
            totals[index] = totals[index] + mm(jnp.where(hit, 1.0, 0.0).astype(BF16), block)
    return totals


def mix_kernel(padded, back_ref, slots_ref, gates_ref, residual_ref, mixed_ref):
    gates = gates_ref[...]
    one, two = gather_stage(back_ref, slots_ref[...], ((0,), (1,)), padded)
    mixed_ref[...] = (
        residual_ref[...] + (gates[:, 0:1] * one + gates[:, 1:2] * two)
    ).astype(BF16)


def third_kernel(
    capacity,
    padded,
    grads_ref,
    slots_ref,
    gates_ref,
    routes_ref,
    cot_ref,
    residual_ref,
    moe_input_ref,
    attended_ref,
    stats_ref,
    query_ref,
    own_ref,
    other_ref,
    lengths_ref,
    pack_ref,
    out_weight_ref,
    residual_grad_ref,
    query_grad_ref,
    own_grad_ref,
    other_grad_ref,
    out_grad_ref,
    small_ref,
    bias_ref,
    attended_grad_ref,
    delta_ref,
):
    rows, width = residual_ref.shape
    head_dim = width // HEADS
    couple = 2 * head_dim
    experts = grads_ref.shape[0]
    pack = pack_ref[...]
    slots, gates, routes = slots_ref[...], gates_ref[...], routes_ref[...]

    def store_bias(half, block):
        bias_ref[half] = block

    bias_stage(lengths_ref, rows, store_bias)
    (moe_grad,) = gather_stage(grads_ref, slots, ((0, 1),), padded)
    place, lane = iota((padded, 128), 0), iota((rows, 128), 1)
    found = [jnp.zeros((rows, 128), F32) for _ in range(2)]
    for expert in range(experts):
        tail = grads_ref[expert][:, 0:128].astype(F32)
        inside = (place >= capacity) & (place < capacity + 3)
        row = jnp.sum(jnp.where(inside, tail, 0.0), axis=0, keepdims=True)
        for k in range(2):
            found[k] = found[k] + jnp.where(
                slots[:, k : k + 1] - expert * padded == lane, row, 0.0
            )
    gate_grad = [jnp.sum(part, axis=1, keepdims=True) for part in found]
    gate = [gates[:, k : k + 1] for k in range(2)]
    inner = gate[0] * gate_grad[0] + gate[1] * gate_grad[1]
    pack_lane = iota((rows, pack.shape[0]), 1)
    logit_grad = sum(
        jnp.where(
            pack_lane == routes[:, k : k + 1] + ROUTER_ROW, gate[k] * (gate_grad[k] - inner), 0.0
        )
        for k in range(2)
    )
    parts = [part.astype(BF16) for part in pieces(logit_grad, 3)]
    moe_input = moe_input_ref[...]
    moe_grad = moe_grad + sum(mm(part, pack) for part in parts)
    router_grad = sum(mm_tn(part, moe_input) for part in parts)
    upstream = cot_ref[...].astype(F32)
    xhat, scale = normalise(residual_ref[...])
    gain_grad = jnp.sum(moe_grad * xhat, axis=0, keepdims=True)
    shift_grad = jnp.sum(moe_grad, axis=0, keepdims=True)
    small_row = iota(small_ref.shape, 0)
    small_ref[...] = jnp.where(
        small_row == 2, gain_grad, jnp.where(small_row == 3, shift_grad, router_grad)
    )
    residual_grad = upstream + norm_backward(moe_grad, pack[2:3].astype(F32), xhat, scale)
    residual_grad_ref[...] = residual_grad
    branch = residual_grad.astype(BF16)
    out_grad_ref[...] = mm_tn(attended_ref[...], branch)
    attended_grad_ref[...] = mm_nt(branch, out_weight_ref[...]).astype(BF16)
    low_lane = iota((1, couple), 1) < head_dim
    pair_refs = (own_ref, other_ref)
    out_refs = (own_grad_ref, other_grad_ref)

    def step(index, _):
        lanes = pl.ds(pl.multiple_of(index * couple, couple), couple)
        value_lanes = pl.ds(pl.multiple_of(width + index * couple, couple), couple)
        query = query_ref[:, lanes].astype(F32) * head_dim**-0.5
        grad = attended_grad_ref[:, lanes].astype(F32)
        query_low, grad_low = query.astype(BF16), grad.astype(BF16)
        keys = [ref[:, lanes] for ref in pair_refs]
        values = [ref[:, value_lanes] for ref in pair_refs]
        keys_turned = [part.astype(F32).T.astype(BF16) for part in keys]
        key_grads = [[], []]
        value_grads = [[], []]
        query_grads = []
        for head in range(2):
            chosen = low_lane == (head == 0)
            mine = jnp.where(chosen, query, 0.0).astype(BF16)
            mine_grad = jnp.where(chosen, grad, 0.0).astype(BF16)
            stats = stats_ref[pl.ds(index * 2 + head, 1), :]
            weighting = [
                jnp.exp(mm_nt(keys[half], mine) + bias_ref[half] - stats) for half in range(2)
            ]
            weighting_grad = [mm_nt(values[half], mine_grad) for half in range(2)]
            delta = sum(
                jnp.sum(weighting[half] * weighting_grad[half], axis=0, keepdims=True)
                for half in range(2)
            )
            here = slice(head * head_dim, (head + 1) * head_dim)
            query_total = 0.0
            for half in range(2):
                scores_grad = (weighting[half] * (weighting_grad[half] - delta)).astype(BF16)
                value_grads[half].append(mm(weighting[half].astype(BF16), grad_low))
                key_grads[half].append(mm(scores_grad, query_low))
                query_total = query_total + mm(keys_turned[half][here], scores_grad)
            query_grads.append(query_total * head_dim**-0.5)
        query_grad_ref[:, lanes] = jnp.concatenate(query_grads, axis=0).T.astype(BF16)
        for half in range(2):
            out_refs[half][:, lanes] = jnp.where(low_lane, *key_grads[half]).astype(
                out_refs[half].dtype
            )
            out_refs[half][:, value_lanes] = jnp.where(low_lane, *value_grads[half]).astype(
                out_refs[half].dtype
            )
        return 0

    lax.fori_loop(0, HEADS // 2, step, 0)


def fourth_kernel(
    tokens_ref,
    pack_ref,
    weight_ref,
    residual_grad_ref,
    query_grad_ref,
    own_grad_ref,
    arrived_grad_ref,
    small_in_ref,
    tokens_grad_ref,
    in_grad_ref,
    small_ref,
    packed_grad,
):
    width = tokens_ref.shape[1]
    pack = pack_ref[...].astype(F32)
    xhat, scale = normalise(tokens_ref[...].astype(F32))
    low = (xhat * pack[0:1] + pack[1:2]).astype(BF16)
    packed_grad[:, 0:width] = query_grad_ref[...]
    packed_grad[:, width:] = (own_grad_ref[...] + arrived_grad_ref[...].astype(F32)).astype(BF16)
    for part in range(3):
        here = slice(part * width, (part + 1) * width)
        in_grad_ref[:, here] = mm_tn(low, packed_grad[:, here])
    first_grad = sum(
        mm_nt(
            packed_grad[:, part * width : (part + 1) * width],
            weight_ref[:, part * width : (part + 1) * width],
        )
        for part in range(3)
    )
    tokens_grad_ref[...] = (
        residual_grad_ref[...] + norm_backward(first_grad, pack[0:1], xhat, scale)
    ).astype(BF16)
    small_row = iota(small_ref.shape, 0)
    small_ref[...] = jnp.where(
        small_row == 0,
        jnp.sum(first_grad * xhat, axis=0, keepdims=True),
        jnp.where(small_row == 1, jnp.sum(first_grad, axis=0, keepdims=True), small_in_ref[...]),
    )


def shape(dims, dtype):
    return jax.ShapeDtypeStruct(dims, dtype)


def call(kernel, outs, specs, scratch=(), name=None, flops=10**9):
    return pl.pallas_call(
        kernel,
        out_shape=outs,
        in_specs=specs,
        out_specs=tuple(VMEM for _ in outs),
        scratch_shapes=scratch,
        compiler_params=pltpu.CompilerParams(vmem_limit_bytes=56 * 2**20),
        cost_estimate=pl.CostEstimate(flops=flops, bytes_accessed=10**7, transcendentals=0),
        name=name,
    )


def body(
    tokens,
    first_gain,
    first_shift,
    attention_in,
    attention_out,
    second_gain,
    second_shift,
    router_weight,
    up_weight,
    down_weight,
    routes,
    priority,
    lengths,
    out_cotangent,
):
    micro_count, _, rows, width = tokens.shape
    experts = lax.axis_size("exp") * up_weight.shape[0]
    hidden_width = up_weight.shape[2]
    capacity = (210 * rows + 100 * experts - 1) // (100 * experts)
    padded = (capacity + 3 + 7) // 8 * 8
    slots_all = experts * padded
    core = lax.axis_index("dp")
    half_seq = lax.axis_index("seq")

    def swap(value, axis):
        return lax.ppermute(value, axis, [(0, 1), (1, 0)])

    def whole(value, axis):
        got = swap(value, "dp")
        return jnp.where(
            core == 0,
            jnp.concatenate([value, got], axis=axis),
            jnp.concatenate([got, value], axis=axis),
        )

    pack_rows = (ROUTER_ROW + experts + 15) // 16 * 16
    norms = jnp.stack([first_gain, first_shift, second_gain, second_shift])
    pack = jnp.concatenate(
        [
            norms,
            jnp.zeros((ROUTER_ROW - 4, norms.shape[1]), BF16),
            router_weight.T,
            jnp.zeros((pack_rows - ROUTER_ROW - experts, norms.shape[1]), BF16),
        ]
    )
    pack = whole(pack, 1)
    in_full = whole(attention_in, 0)
    out_full = whole(attention_out, 0)
    up_full = whole(up_weight[0], 0)
    down_full = whole(down_weight[0], 0)

    block = (experts, padded, width)

    def exchange(value):
        return lax.all_to_all(value, "exp", split_axis=0, concat_axis=0, tiled=True)

    slots, cots, queries, pairs, got_pairs = [], [], [], [], []
    for m in range(micro_count):
        slot, sent = call(
            partial(dispatch_kernel, capacity, padded),
            (shape((rows, 2), jnp.int32), shape(block, BF16)),
            [VMEM] * 3,
            name="claim_slots",
        )(routes[m, 0], priority[m], out_cotangent[m, 0])
        slots.append(slot)
        cots.append(exchange(sent))
        query, pair = call(
            first_kernel,
            (shape((rows, width), BF16), shape((rows, 2 * width), BF16)),
            [VMEM] * 3,
            name="project_in",
        )(tokens[m, 0], pack, in_full)
        queries.append(query)
        pairs.append(pair)
        got_pairs.append(swap(pair, "seq"))
    residuals, moe_inputs, attendeds, statses, gateses, arrived = [], [], [], [], [], []
    for m in range(micro_count):
        residual, moe_input, attended, stats, gates, sent = call(
            partial(second_kernel, capacity, padded),
            (
                shape((rows, width), F32),
                shape((rows, width), BF16),
                shape((rows, width), BF16),
                shape((16, rows), F32),
                shape((rows, 2), F32),
                shape(block, BF16),
            ),
            [VMEM] * 5 + [SMEM] + [VMEM] * 3,
            (pltpu.VMEM((2, rows, rows), F32),),
            name="attend",
        )(
            tokens[m, 0],
            pack,
            queries[m],
            pairs[m],
            got_pairs[m],
            lengths[m, 0],
            out_full,
            routes[m, 0],
            slots[m],
        )
        residuals.append(residual)
        moe_inputs.append(moe_input)
        attendeds.append(attended)
        statses.append(stats)
        gateses.append(gates)
        arrived.append(exchange(sent))
    chunk = 256
    chunks = hidden_width // chunk
    up_sum = down_sum = None
    backs, grads = [], []
    whole_block = pl.BlockSpec(block, lambda i: (0, 0, 0))
    up_spec = pl.BlockSpec((width, chunk), lambda i: (0, i))
    down_spec = pl.BlockSpec((chunk, width), lambda i: (i, 0))
    for m in range(micro_count):
        old = () if m == 0 else (up_sum, down_sum)
        back, grad, up_sum, down_sum = pl.pallas_call(
            partial(expert_kernel, capacity, padded, chunks, m == 0),
            out_shape=(
                shape(block, BF16),
                shape(block, BF16),
                shape((width, hidden_width), F32),
                shape((hidden_width, width), F32),
            ),
            grid=(chunks,),
            in_specs=[whole_block, whole_block, up_spec, down_spec]
            + ([] if m == 0 else [up_spec, down_spec]),
            out_specs=(whole_block, whole_block, up_spec, down_spec),
            scratch_shapes=[
                pltpu.VMEM((slots_all, width), BF16),
                pltpu.VMEM((width, slots_all), BF16),
                pltpu.VMEM((slots_all, width), BF16),
                pltpu.VMEM((slots_all, width), F32),
                pltpu.VMEM((slots_all, width), F32),
            ],
            compiler_params=pltpu.CompilerParams(vmem_limit_bytes=56 * 2**20),
            cost_estimate=pl.CostEstimate(
                flops=12 * slots_all * width * hidden_width,
                bytes_accessed=10**7,
                transcendentals=0,
            ),
            name="expert",
        )(arrived[m], cots[m], up_full, down_full, *old)
        backs.append(exchange(back))
        grads.append(exchange(grad))
    mixed_parts, token_grads = [], []
    in_sum = out_sum = small_sum = 0.0
    for m in range(micro_count):
        residual_grad, query_grad, own_grad, other_grad, out_grad, small = call(
            partial(third_kernel, capacity, padded),
            (
                shape((rows, width), F32),
                shape((rows, width), BF16),
                shape((rows, 2 * width), F32),
                shape((rows, 2 * width), BF16),
                shape((width, width), F32),
                shape((pack_rows, width), F32),
            ),
            [VMEM] * 12 + [SMEM] + [VMEM] * 2,
            (
                pltpu.VMEM((2, rows, rows), F32),
                pltpu.VMEM((rows, width), BF16),
                pltpu.VMEM((16, rows), F32),
            ),
            name="attend_back",
        )(
            grads[m],
            slots[m],
            gateses[m],
            routes[m, 0],
            out_cotangent[m, 0],
            residuals[m],
            moe_inputs[m],
            attendeds[m],
            statses[m],
            queries[m],
            pairs[m],
            got_pairs[m],
            lengths[m, 0],
            pack,
            out_full,
        )
        got_grad = swap(other_grad, "seq")
        (mixed,) = call(
            partial(mix_kernel, padded), (shape((rows, width), BF16),), [VMEM] * 4, name="mix"
        )(backs[m], slots[m], gateses[m], residuals[m])
        mixed_parts.append(mixed)
        tokens_grad, in_grad, small = call(
            fourth_kernel,
            (
                shape((rows, width), BF16),
                shape((width, 3 * width), F32),
                shape((pack_rows, width), F32),
            ),
            [VMEM] * 8,
            (pltpu.VMEM((rows, 3 * width), BF16),),
            name="project_back",
        )(
            tokens[m, 0],
            pack,
            in_full,
            residual_grad,
            query_grad,
            own_grad,
            got_grad,
            small,
        )
        token_grads.append(tokens_grad)
        in_sum = in_sum + in_grad
        out_sum = out_sum + out_grad
        small_sum = small_sum + small

    def halves(value, axis):
        size = value.shape[axis] // 2
        mine = lax.dynamic_slice_in_dim(value, core * size, size, axis)
        theirs = lax.dynamic_slice_in_dim(value, (1 - core) * size, size, axis)
        return mine + swap(theirs.astype(BF16), "dp").astype(F32)

    def pair_sum(value):
        low = value.astype(BF16)
        return low.astype(F32) + swap(low, "seq").astype(F32)

    up_total = pair_sum(halves(up_sum, 0))[None]
    down_total = pair_sum(halves(down_sum, 0))[None]
    dense = halves(jnp.concatenate([in_sum, out_sum], axis=1), 0).astype(BF16)
    dense = lax.psum(dense, ("seq", "exp")).astype(F32)
    small = halves(small_sum, 1)
    small = lax.psum(small, ("seq", "exp"))
    return (
        jnp.stack(mixed_parts)[:, None],
        jnp.stack(token_grads)[:, None],
        small[0],
        small[1],
        dense[:, : 3 * width],
        dense[:, 3 * width :],
        small[2],
        small[3],
        small[ROUTER_ROW : ROUTER_ROW + experts].T,
        up_total,
        down_total,
    )


def solution(mesh):
    placed = (
        P(None, ("exp", "dp"), "seq", None),
        P("dp"),
        P("dp"),
        P("dp", None),
        P("dp", None),
        P("dp"),
        P("dp"),
        P("dp", None),
        P("exp", "dp", None),
        P("exp", "dp", None),
        P(None, ("exp", "dp"), "seq", None),
        P(None, ("exp", "dp"), "seq"),
        P(None, ("exp", "dp"), None),
        P(None, ("exp", "dp"), "seq", None),
    )
    return jax.shard_map(
        body,
        mesh=mesh,
        in_specs=placed,
        out_specs=(
            P(None, ("exp", "dp"), "seq", None),
            P(None, ("exp", "dp"), "seq", None),
            P("dp"),
            P("dp"),
            P("dp", None),
            P("dp", None),
            P("dp"),
            P("dp"),
            P("dp", None),
            P("exp", "dp", None),
            P("exp", "dp", None),
        ),
        check_vma=False,
    )
```

time: 1210 us -> 616 us (0.51)
  blocking collectives: 408 us -> 112 us
  Pallas kernels: 0 us -> 218 us
  matrix products: 212 us -> 0 us
  other arithmetic: 166 us -> 56.3 us
  waiting for transfers between devices: 227 us -> 118 us
  local copies, waits for them, and re-layouts: 135 us -> 31 us
  starting transfers between devices: 38.8 us -> 57 us
    psum x1, blocking collectives: 395 us -> 78.4 us  [body(): small = lax.psum(small, ('seq', 'exp'))]
    pallas_call x0 -> x14, Pallas kernels: none -> 218 us  [the longest x2 92.4 us: body(): pl.pallas_call(partial(expert_kernel, capacity, padded, chunks, m == 0),...]
    dot_general x42 -> x0, matrix products: 212 us -> none  [the longest x2 25 us: body(): jnp.einsum('ecd,fd->ecf', at_expert, down_full[0], preferred_element_type...]
    psum x1, waiting for transfers between devices: 120 us -> 27.8 us  [body(): dense = lax.psum(dense, ('seq', 'exp')).astype(F32)]
    convert_element_type x21 -> x4, other arithmetic: 84.7 us -> 16.2 us  [the longest x2 10.5 us: pair_sum(): low = value.astype(BF16)]
    ppermute x0 -> x15, waiting for transfers between devices: none -> 64 us  [swap(): return lax.ppermute(value, axis, [(0, 1), (1, 0)])]
    all_gather x6 -> x0, waiting for transfers between devices: 46.9 us -> none  [the longest x2 36.3 us: body(): pairs = lax.all_gather(packed[:, width:], 'seq', axis=0, tiled=True)]
    reduce_sum x25 -> x0, other arithmetic: 46.6 us -> none  [the longest x2 9.51 us: body(): jnp.sum(gate[:, :, None] * chosen_rows, axis=1)]
  transfers between devices with their start and end apart: 22 -> 23, of which waited for: 11 -> 7; matrix products, arithmetic and copies ran while one was open for 34% -> 12% of each run, Pallas kernels for 0% -> 35%
where the time goes in v1:
time: 616 us; the launch traced here: 607 us
  Pallas kernels  218 us (35%)
  waiting for transfers between devices  118 us (19%)
  blocking collectives  112 us (18%)
  starting transfers between devices  57 us (9%)
  other arithmetic  56.3 us (9%)
  local copies, waits for them, and re-layouts  31 us (5%)
  between operations  14.7 us (2%)
    pallas_call x2, Pallas kernels, body(): pl.pallas_call(partial(expert_kernel, capacity, padded, chunks, m == 0),...  92.4 us
    psum x1, blocking collectives, body(): small = lax.psum(small, ('seq', 'exp'))  78.4 us
    ppermute x15, waiting for transfers between devices, swap(): return lax.ppermute(value, axis, [(0, 1), (1, 0)])  64 us
    pallas_call x2, Pallas kernels, body(): call(partial(third_kernel, capacity, padded), (shape((rows, width), F32),...  51.1 us
    all_to_all x7, starting transfers between devices, exchange(): return lax.all_to_all(value, 'exp', split_axis=0, concat_axis=0, tiled=True)  48.4 us
    all_to_all x1, blocking collectives, exchange(): return lax.all_to_all(value, 'exp', split_axis=0, concat_axis=0, tiled=True)  34.1 us
    pallas_call x2, Pallas kernels, body(): call(partial(second_kernel, capacity, padded), (shape((rows, width), F32)...  28.8 us
    psum x1, waiting for transfers between devices, body(): dense = lax.psum(dense, ('seq', 'exp')).astype(F32)  27.8 us
  transfers between devices with their start and end apart: 23, of which 7 were waited for; matrix products, arithmetic and copies ran while one was open for 12% of the time, Pallas kernels for 35%

profile of v1, /device:TPU:0, one launch (start us, length us, event | category | flops | bytes accessed | tf_op | source)
XLA Modules:
  0.0 607.3 jit_solution(6876215314937867463)
XLA Ops:
  15.7 7.3 %all-to-all-start.1 = ((bf16[8,104,768]{2,1,0:T(8,128)(2,1)}), bf16[8,104,768]{2,1,0:T(8,128)(2,1)}, u32[]{:S(2)}, u32[]{:S(2)}) async-start(bf16[8,104,768]{2,1,0:T(8,128)(2,1)} %get-tuple-element.61), calls=%async_computation.1 | async-start | bytes 2555904 | tf_op jit(solution)/shard_map/all_to_all | solution.py:631
  27.9 25.9 %all-to-all-done.1.cot_ref = bf16[8,104,768]{2,1,0:T(8,128)(2,1)} async-done(((bf16[8,104,768]{2,1,0:T(8,128)(2,1)}), bf16[8,104,768]{2,1,0:T(8,128)(2,1)}, u32[]{:S(2)}, u32[]{:S(2)}) %all-to-all-start.1) | async-done | bytes 1277984 | tf_op jit(solution)/shard_map/all_to_all | solution.py:631
  53.8 4.3 all-to-all-start.4
  67.8 5.1 project_in.2
  77.9 23.6 %collective-permute-done.2.other_ref = bf16[384,1536]{1,0:T(8,128)(2,1)S(1)} collective-permute-done((bf16[384,1536]{1,0:T(8,128)(2,1)}, bf16[384,1536]{1,0:T(8,128)(2,1)S(1)}, u32[]{:S(2)}, u32[]{:S(2)}) %collective-permute-start.2) | collective-permute-done | bytes 1179680 | tf_op jit(solution)/shard_map/ppermute | solution.py:602
  102.5 14.4 %attend.2 = (f32[384,768]{1,0:T(8,128)}, bf16[384,768]{1,0:T(8,128)(2,1)}, bf16[384,768]{1,0:T(8,128)(2,1)}, f32[16,384]{1,0:T(8,128)}, f32[384,2]{1,0:T(8,128)}, /*index=5*/bf16[8,104,768]{2,1,0:T(8,128)(2,1)}) custom-call(bf16[384,768]{1,0:T(8,128)(2,1)} %get-tuple-element.120.tokens_ref, bf16[16,768]{1,0:T(8,128)(2,1)} %maximum_select_fusion.4.pack_ref, ...), custom_call_target="tpu_custom_call" | custom-call | flops 1000000000 | bytes 10000000 | tf_op jit(solution)/shard_map/attend/pallas_call | solution.py:654
  116.9 6.2 %all-to-all-start = ((bf16[8,104,768]{2,1,0:T(8,128)(2,1)}), bf16[8,104,768]{2,1,0:T(8,128)(2,1)S(1)}, u32[]{:S(2)}, u32[]{:S(2)}) async-start(bf16[8,104,768]{2,1,0:T(8,128)(2,1)} %get-tuple-element.60), calls=%async_computation | async-start | bytes 2555904 | tf_op jit(solution)/shard_map/all_to_all | solution.py:631
  123.1 5.0 project_in.3
  129.7 7.7 %maximum_select_fusion.up_ref = bf16[768,3072]{1,0:T(8,128)(2,1)} fusion(bf16[384,3072]{1,0:T(8,128)(2,1)} %collective-permute-done.4, bf16[384,3072]{1,0:T(8,128)(2,1)} %bitcast.6, pred[]{:T(512)S(6)} %eq.2), kind=kLoop, calls=%fused_computation.9 | loop fusion | flops 21233664 | bytes 9437185 | tf_op jit(solution)/shard_map/jit(_where)/select_n | solution.py:606
  137.4 18.3 %collective-permute-done.6.other_ref = bf16[384,1536]{1,0:T(8,128)(2,1)S(1)} collective-permute-done((bf16[384,1536]{1,0:T(8,128)(2,1)}, bf16[384,1536]{1,0:T(8,128)(2,1)S(1)}, u32[]{:S(2)}, u32[]{:S(2)}) %collective-permute-start.6) | collective-permute-done | bytes 1179680 | tf_op jit(solution)/shard_map/ppermute | solution.py:602
  156.7 14.4 %attend.3 = (f32[384,768]{1,0:T(8,128)}, bf16[384,768]{1,0:T(8,128)(2,1)}, bf16[384,768]{1,0:T(8,128)(2,1)}, f32[16,384]{1,0:T(8,128)}, f32[384,2]{1,0:T(8,128)}, /*index=5*/bf16[8,104,768]{2,1,0:T(8,128)(2,1)}) custom-call(bf16[384,768]{1,0:T(8,128)(2,1)} %get-tuple-element.121.tokens_ref, bf16[16,768]{1,0:T(8,128)(2,1)} %maximum_select_fusion.4.pack_ref, ...), custom_call_target="tpu_custom_call" | custom-call | flops 1000000000 | bytes 10000000 | tf_op jit(solution)/shard_map/attend/pallas_call | solution.py:654
  171.1 5.7 all-to-all-start.3
  176.9 7.1 %maximum_select_fusion.1.down_ref = bf16[3072,768]{1,0:T(8,128)(2,1)} fusion(bf16[1536,768]{1,0:T(8,128)(2,1)} %collective-permute-done.5, bf16[1536,768]{1,0:T(8,128)(2,1)} %bitcast.7, pred[]{:T(512)S(6)} %eq.2), kind=kLoop, calls=%fused_computation.10 | loop fusion | flops 21233664 | bytes 9437185 | tf_op jit(solution)/shard_map/jit(_where)/select_n | solution.py:606
  184.0 45.8 %expert.2 = (bf16[8,104,768]{2,1,0:T(8,128)(2,1)}, bf16[8,104,768]{2,1,0:T(8,128)(2,1)}, f32[768,3072]{1,0:T(8,128)}, f32[3072,768]{1,0:T(8,128)}) custom-call(bf16[8,104,768]{2,1,0:T(8,128)(2,1)} %copy-done.9, bf16[8,104,768]{2,1,0:T(8,128)(2,1)} %all-to-all-done.1.cot_ref, bf16[768,3072]{1,0:T(8,128)(2,1)} %maximum_select_fusion.up_ref, ...), custom_call_target="tpu_custom_call" | custom-call | flops 23555211264 | bytes 10000000 | tf_op jit(solution)/shard_map/expert/pallas_call | solution.py:693
  229.7 6.0 all-to-all-start.6
  235.7 46.6 %expert.3 = (bf16[8,104,768]{2,1,0:T(8,128)(2,1)}, bf16[8,104,768]{2,1,0:T(8,128)(2,1)}, f32[768,3072]{1,0:T(8,128)}, f32[3072,768]{1,0:T(8,128)}) custom-call(bf16[8,104,768]{2,1,0:T(8,128)(2,1)} %copy-done.10, bf16[8,104,768]{2,1,0:T(8,128)(2,1)} %all-to-all-done.4.cot_ref, bf16[768,3072]{1,0:T(8,128)(2,1)} %maximum_select_fusion.up_ref, ...), custom_call_target="tpu_custom_call" | custom-call | flops 23555211264 | bytes 10000000 | tf_op jit(solution)/shard_map/expert/pallas_call | solution.py:693
  282.4 34.1 %all_to_all.40.grads_ref = bf16[8,104,768]{2,1,0:T(8,128)(2,1)} all-to-all(bf16[8,104,768]{2,1,0:T(8,128)(2,1)} %get-tuple-element.85), channel_id=1, replica_groups=mesh['seq'=2,'exp'=8,'dp'=2] {'exp'}, dimensions={0} | all-to-all | bytes 2555904 | tf_op jit(solution)/shard_map/all_to_all | solution.py:631
  316.5 13.0 %all-to-all-start.2 = ((bf16[8,104,768]{2,1,0:T(8,128)(2,1)}), bf16[8,104,768]{2,1,0:T(8,128)(2,1)S(1)}, u32[]{:S(2)}, u32[]{:S(2)}) async-start(bf16[8,104,768]{2,1,0:T(8,128)(2,1)} %get-tuple-element.62), calls=%async_computation.2 | async-start | bytes 2555904 | tf_op jit(solution)/shard_map/all_to_all | solution.py:631
  329.5 25.5 %attend_back.2 = (f32[384,768]{1,0:T(8,128)}, bf16[384,768]{1,0:T(8,128)(2,1)}, f32[384,1536]{1,0:T(8,128)}, bf16[384,1536]{1,0:T(8,128)(2,1)}, f32[768,768]{1,0:T(8,128)}, /*index=5*/f32[16,768]{1,0:T(8,128)}) custom-call(bf16[8,104,768]{2,1,0:T(8,128)(2,1)} %copy-done.2, s32[384,2]{1,0:T(8,128)} %get-tuple-element.59.slots_ref, ...), custom_call_target="tpu_custom_call" | custom-call | flops 1000000000 | bytes 10000000 | tf_op jit(solution)/shard_map/attend_back/pallas_call | solution.py:725
  356.6 25.6 %attend_back.3 = (f32[384,768]{1,0:T(8,128)}, bf16[384,768]{1,0:T(8,128)(2,1)}, f32[384,1536]{1,0:T(8,128)}, bf16[384,1536]{1,0:T(8,128)(2,1)}, f32[768,768]{1,0:T(8,128)}, /*index=5*/f32[16,768]{1,0:T(8,128)}) custom-call(bf16[8,104,768]{2,1,0:T(8,128)(2,1)} %all_to_all.40.grads_ref, s32[384,2]{1,0:T(8,128)} %get-tuple-element.67.slots_ref, ...), custom_call_target="tpu_custom_call" | custom-call | flops 1000000000 | bytes 10000000 | tf_op jit(solution)/shard_map/attend_back/pallas_call | solution.py:725
  382.8 5.9 all-to-all-start.5
  392.9 4.3 dynamic-slice_convert_fusion.1
  398.0 9.7 %project_back.2 = (bf16[384,768]{1,0:T(8,128)(2,1)}, f32[768,2304]{1,0:T(8,128)}, f32[16,768]{1,0:T(8,128)}) custom-call(bf16[384,768]{1,0:T(8,128)(2,1)} %get-tuple-element.120.tokens_ref, bf16[16,768]{1,0:T(8,128)(2,1)} %maximum_select_fusion.4.pack_ref, bf16[768,2304]{1,0:T(8,128)(2,1)} %maximum_select_fusion.2.weight_ref, ...), custom_call_target="tpu_custom_call" | custom-call | flops 1000000000 | bytes 10000000 | tf_op jit(solution)/shard_map/project_back/pallas_call | solution.py:764
  408.4 9.6 %project_back.3 = (bf16[384,768]{1,0:T(8,128)(2,1)}, f32[768,2304]{1,0:T(8,128)}, f32[16,768]{1,0:T(8,128)}) custom-call(bf16[384,768]{1,0:T(8,128)(2,1)} %get-tuple-element.121.tokens_ref, bf16[16,768]{1,0:T(8,128)(2,1)} %maximum_select_fusion.4.pack_ref, bf16[768,2304]{1,0:T(8,128)(2,1)} %maximum_select_fusion.2.weight_ref, ...), custom_call_target="tpu_custom_call" | custom-call | flops 1000000000 | bytes 10000000 | tf_op jit(solution)/shard_map/project_back/pallas_call | solution.py:764
  418.0 5.9 add.51
  438.1 5.1 add_convert_fusion
  444.1 5.3 add_convert_fusion.1
  456.8 78.4 %psum.14 = f32[16,384]{1,0:T(8,128)S(1)} all-reduce(f32[16,384]{1,0:T(8,128)S(1)} %convert_add_fusion), channel_id=1, replica_groups=mesh['seq'=2,'exp'=8,'dp'=2] {'seq','exp'}, use_global_device_ids=true, to_apply=%region_0.1 | all-reduce | flops 6144 | bytes 49152 | tf_op jit(solution)/shard_map/psum | solution.py:804
  536.4 5.1 add_bitcast_fusion
  541.5 20.5 %collective-permute-done.12 = bf16[384,3072]{1,0:T(8,128)(2,1)} collective-permute-done((bf16[384,3072]{1,0:T(8,128)(2,1)}, bf16[384,3072]{1,0:T(8,128)(2,1)}, u32[]{:S(2)}, u32[]{:S(2)}) %collective-permute-start.12) | collective-permute-done | bytes 2359328 | tf_op jit(solution)/shard_map/ppermute | solution.py:602
  562.0 5.4 add_bitcast_fusion.1
  567.5 27.8 %all-reduce.2.cloned.1.call-done = bf16[384,3072]{1,0:T(8,128)(2,1)} async-done(((bf16[384,3072]{1,0:T(8,128)(2,1)}), bf16[384,3072]{1,0:T(8,128)(2,1)}) %all-reduce.2.cloned.1.call-update) | async-done | bytes 2359312 | tf_op jit(solution)/shard_map/psum | solution.py:802
  (119 shorter events, 67.9 us)
Async XLA Ops:
  11.6 11.4 %copy-start.7 = (bf16[384,2304]{1,0:T(8,128)(2,1)S(1)}, bf16[384,2304]{1,0:T(8,128)(2,1)}, u32[]{:S(2)}) copy-start(bf16[384,2304]{1,0:T(8,128)(2,1)} %param.17) | copy-start | bytes 5308420
  15.7 38.1 %all-to-all-start.1 = ((bf16[8,104,768]{2,1,0:T(8,128)(2,1)}), bf16[8,104,768]{2,1,0:T(8,128)(2,1)}, u32[]{:S(2)}, u32[]{:S(2)}) async-start(bf16[8,104,768]{2,1,0:T(8,128)(2,1)} %get-tuple-element.61), calls=%async_computation.1 | async-start | bytes 2555904 | tf_op jit(solution)/shard_map/all_to_all | solution.py:631
  23.0 42.6 %collective-permute-start.1 = (bf16[384,2304]{1,0:T(8,128)(2,1)S(1)}, bf16[384,2304]{1,0:T(8,128)(2,1)S(1)}, u32[]{:S(2)}, u32[]{:S(2)}) collective-permute-start(bf16[384,2304]{1,0:T(8,128)(2,1)S(1)} %copy-done.7), channel_id=1, source_target_pairs={{0,1},{1,0},{2,3},{3,2},{4,5},{5,4},{6,7},{7,6},{8,9},{9,8},{10,11... | collective-permute-start | bytes 5308424 | tf_op jit(solution)/shard_map/ppermute | solution.py:602
  23.9 34.2 %copy-start.18 = (bf16[384]{0:T(512)(128)(2,1)S(1)}, bf16[384]{0:T(512)(128)(2,1)}, u32[]{:S(2)}) copy-start(bf16[384]{0:T(512)(128)(2,1)} %param.15) | copy-start | bytes 2308
  23.9 34.7 %copy-start.19 = (bf16[384]{0:T(512)(128)(2,1)S(1)}, bf16[384]{0:T(512)(128)(2,1)}, u32[]{:S(2)}) copy-start(bf16[384]{0:T(512)(128)(2,1)} %param.16) | copy-start | bytes 2308
  23.9 35.3 %copy-start.20 = (bf16[384]{0:T(512)(128)(2,1)S(1)}, bf16[384]{0:T(512)(128)(2,1)}, u32[]{:S(2)}) copy-start(bf16[384]{0:T(512)(128)(2,1)} %param.19) | copy-start | bytes 2308
  23.9 35.9 %copy-start.21 = (bf16[384]{0:T(512)(128)(2,1)S(1)}, bf16[384]{0:T(512)(128)(2,1)}, u32[]{:S(2)}) copy-start(bf16[384]{0:T(512)(128)(2,1)} %param.20) | copy-start | bytes 2308
  53.8 63.1 %all-to-all-start.4 = ((bf16[8,104,768]{2,1,0:T(8,128)(2,1)}), bf16[8,104,768]{2,1,0:T(8,128)(2,1)}, u32[]{:S(2)}, u32[]{:S(2)}) async-start(bf16[8,104,768]{2,1,0:T(8,128)(2,1)} %get-tuple-element.69), calls=%async_computation.4 | async-start | bytes 2555904 | tf_op jit(solution)/shard_map/all_to_all | solution.py:631
  61.8 2.4 collective-permute-start
  72.9 28.6 %collective-permute-start.2 = (bf16[384,1536]{1,0:T(8,128)(2,1)}, bf16[384,1536]{1,0:T(8,128)(2,1)S(1)}, u32[]{:S(2)}, u32[]{:S(2)}) collective-permute-start(bf16[384,1536]{1,0:T(8,128)(2,1)} %get-tuple-element.58.own_ref), channel_id=1, source_target_pairs={{0,16},{16,0},{1,17},{17,1},{2,18},{18,2},{3,19},{19,3},{4,20},{20... | collective-permute-start | bytes 3538952 | tf_op jit(solution)/shard_map/ppermute | solution.py:602
  74.4 2.0 collective-permute-start.3
  74.6 55.0 %collective-permute-start.4 = (bf16[384,3072]{1,0:T(8,128)(2,1)}, bf16[384,3072]{1,0:T(8,128)(2,1)}, u32[]{:S(2)}, u32[]{:S(2)}) collective-permute-start(bf16[384,3072]{1,0:T(8,128)(2,1)} %bitcast.6), channel_id=1, source_target_pairs={{0,1},{1,0},{2,3},{3,2},{4,5},{5,4},{6,7},{7,6},{8,9},{9,8},{10,11... | collective-permute-start | bytes 7077896 | tf_op jit(solution)/shard_map/ppermute | solution.py:602
  74.9 102.0 %collective-permute-start.5 = (bf16[1536,768]{1,0:T(8,128)(2,1)}, bf16[1536,768]{1,0:T(8,128)(2,1)}, u32[]{:S(2)}, u32[]{:S(2)}) collective-permute-start(bf16[1536,768]{1,0:T(8,128)(2,1)} %bitcast.7), channel_id=1, source_target_pairs={{0,1},{1,0},{2,3},{3,2},{4,5},{5,4},{6,7},{7,6},{8,9},{9,8},{10,11... | collective-permute-start | bytes 7077896 | tf_op jit(solution)/shard_map/ppermute | solution.py:602
  116.9 54.2 %all-to-all-start = ((bf16[8,104,768]{2,1,0:T(8,128)(2,1)}), bf16[8,104,768]{2,1,0:T(8,128)(2,1)S(1)}, u32[]{:S(2)}, u32[]{:S(2)}) async-start(bf16[8,104,768]{2,1,0:T(8,128)(2,1)} %get-tuple-element.60), calls=%async_computation | async-start | bytes 2555904 | tf_op jit(solution)/shard_map/all_to_all | solution.py:631
  128.2 27.5 %collective-permute-start.6 = (bf16[384,1536]{1,0:T(8,128)(2,1)}, bf16[384,1536]{1,0:T(8,128)(2,1)S(1)}, u32[]{:S(2)}, u32[]{:S(2)}) collective-permute-start(bf16[384,1536]{1,0:T(8,128)(2,1)} %get-tuple-element.66.own_ref), channel_id=1, source_target_pairs={{0,16},{16,0},{1,17},{17,1},{2,18},{18,2},{3,19},{19,3},{4,20},{20... | collective-permute-start | bytes 3538952 | tf_op jit(solution)/shard_map/ppermute | solution.py:602
  171.1 12.8 %copy-start.9 = (bf16[8,104,768]{2,1,0:T(8,128)(2,1)}, bf16[8,104,768]{2,1,0:T(8,128)(2,1)S(1)}, u32[]{:S(2)}) copy-start(bf16[8,104,768]{2,1,0:T(8,128)(2,1)S(1)} %all-to-all-done.rows_ref) | copy-start | bytes 3833860
  171.1 58.6 %all-to-all-start.3 = ((bf16[8,104,768]{2,1,0:T(8,128)(2,1)}), bf16[8,104,768]{2,1,0:T(8,128)(2,1)S(1)}, u32[]{:S(2)}, u32[]{:S(2)}) async-start(bf16[8,104,768]{2,1,0:T(8,128)(2,1)} %get-tuple-element.68), calls=%async_computation.3 | async-start | bytes 2555904 | tf_op jit(solution)/shard_map/all_to_all | solution.py:631
  229.7 52.7 %all-to-all-start.6 = ((bf16[8,104,768]{2,1,0:T(8,128)(2,1)}), bf16[8,104,768]{2,1,0:T(8,128)(2,1)S(1)}, u32[]{:S(2)}, u32[]{:S(2)}) async-start(bf16[8,104,768]{2,1,0:T(8,128)(2,1)} %get-tuple-element.75), calls=%async_computation.6 | async-start | bytes 2555904 | tf_op jit(solution)/shard_map/all_to_all | solution.py:631
  282.4 34.1 %copy-start.2 = (bf16[8,104,768]{2,1,0:T(8,128)(2,1)}, bf16[8,104,768]{2,1,0:T(8,128)(2,1)S(1)}, u32[]{:S(2)}) copy-start(bf16[8,104,768]{2,1,0:T(8,128)(2,1)S(1)} %all-to-all-done.6.grads_ref) | copy-start | bytes 3833860
  316.5 66.3 %all-to-all-start.2 = ((bf16[8,104,768]{2,1,0:T(8,128)(2,1)}), bf16[8,104,768]{2,1,0:T(8,128)(2,1)S(1)}, u32[]{:S(2)}, u32[]{:S(2)}) async-start(bf16[8,104,768]{2,1,0:T(8,128)(2,1)} %get-tuple-element.62), calls=%async_computation.2 | async-start | bytes 2555904 | tf_op jit(solution)/shard_map/all_to_all | solution.py:631
  355.1 43.0 %collective-permute-start.7 = (bf16[384,1536]{1,0:T(8,128)(2,1)}, bf16[384,1536]{1,0:T(8,128)(2,1)}, u32[]{:S(2)}, u32[]{:S(2)}) collective-permute-start(bf16[384,1536]{1,0:T(8,128)(2,1)} %get-tuple-element.82), channel_id=1, source_target_pairs={{0,16},{16,0},{1,17},{17,1},{2,18},{18,2},{3,19},{19,3},{4,20},{20... | collective-permute-start | bytes 3538952 | tf_op jit(solution)/shard_map/ppermute | solution.py:602
  382.2 26.2 %collective-permute-start.8 = (bf16[384,1536]{1,0:T(8,128)(2,1)}, bf16[384,1536]{1,0:T(8,128)(2,1)}, u32[]{:S(2)}, u32[]{:S(2)}) collective-permute-start(bf16[384,1536]{1,0:T(8,128)(2,1)} %get-tuple-element.92), channel_id=1, source_target_pairs={{0,16},{16,0},{1,17},{17,1},{2,18},{18,2},{3,19},{19,3},{4,20},{20... | collective-permute-start | bytes 3538952 | tf_op jit(solution)/shard_map/ppermute | solution.py:602
  382.8 10.1 %copy-start.8 = (bf16[8,104,768]{2,1,0:T(8,128)(2,1)}, bf16[8,104,768]{2,1,0:T(8,128)(2,1)S(1)}, u32[]{:S(2)}) copy-start(bf16[8,104,768]{2,1,0:T(8,128)(2,1)S(1)} %all-to-all-done.2.back_ref) | copy-start | bytes 3833860
  382.8 48.7 %all-to-all-start.5 = ((bf16[8,104,768]{2,1,0:T(8,128)(2,1)}), bf16[8,104,768]{2,1,0:T(8,128)(2,1)}, u32[]{:S(2)}, u32[]{:S(2)}) async-start(bf16[8,104,768]{2,1,0:T(8,128)(2,1)} %get-tuple-element.72), calls=%async_computation.5 | async-start | bytes 2555904 | tf_op jit(solution)/shard_map/all_to_all | solution.py:631
  388.7 206.6 %all-reduce.2.cloned.1.call-start = ((), (), s32[]{:S(2)}) async-start(), calls=%async_computation.8 | async-start | bytes 4718592 | tf_op jit(solution)/shard_map/psum | solution.py:802
  392.9 45.2 %collective-permute-start.13 = (bf16[1536,768]{1,0:T(8,128)(2,1)}, bf16[1536,768]{1,0:T(8,128)(2,1)}, u32[]{:S(2)}, u32[]{:S(2)}) collective-permute-start(bf16[1536,768]{1,0:T(8,128)(2,1)} %dynamic-slice_convert_fusion), channel_id=1, source_target_pairs={{0,1},{1,0},{2,3},{3,2},{4,5},{5,4},{6,7},{7,6},{8,9},{9,8},{10,11... | collective-permute-start | bytes 7077896 | tf_op jit(solution)/shard_map/ppermute | solution.py:602
  397.2 46.8 %collective-permute-start.11 = (bf16[384,3072]{1,0:T(8,128)(2,1)}, bf16[384,3072]{1,0:T(8,128)(2,1)}, u32[]{:S(2)}, u32[]{:S(2)}) collective-permute-start(bf16[384,3072]{1,0:T(8,128)(2,1)} %dynamic-slice_convert_fusion.1), channel_id=1, source_target_pairs={{0,1},{1,0},{2,3},{3,2},{4,5},{5,4},{6,7},{7,6},{8,9},{9,8},{10,11... | collective-permute-start | bytes 7077896 | tf_op jit(solution)/shard_map/ppermute | solution.py:602
  427.4 23.2 %collective-permute-start.10 = (bf16[384,3072]{1,0:T(8,128)(2,1)}, bf16[384,3072]{1,0:T(8,128)(2,1)}, u32[]{:S(2)}, u32[]{:S(2)}) collective-permute-start(bf16[384,3072]{1,0:T(8,128)(2,1)} %fusion.1), channel_id=1, source_target_pairs={{0,1},{1,0},{2,3},{3,2},{4,5},{5,4},{6,7},{7,6},{8,9},{9,8},{10,11... | collective-permute-start | bytes 7077896 | tf_op jit(solution)/shard_map/ppermute | solution.py:602
  438.1 12.5 %slice-start = ((s8[7077888]{0:T(1024)(128)(4,1)}), s8[4194304]{0:T(1024)(128)(4,1)S(1)}, s32[]{:S(2)}) async-start(s8[7077888]{0:T(1024)(128)(4,1)} %bitcast.39), calls=%async_computation.9 | async-start | bytes 8388608
  443.3 93.1 %collective-permute-start.14 = (bf16[1536,768]{1,0:T(8,128)(2,1)}, bf16[1536,768]{1,0:T(8,128)(2,1)}, u32[]{:S(2)}, u32[]{:S(2)}) collective-permute-start(bf16[1536,768]{1,0:T(8,128)(2,1)} %add_convert_fusion), channel_id=1, source_target_pairs={{0,16},{16,0},{1,17},{17,1},{2,18},{18,2},{3,19},{19,3},{4,20},{20... | collective-permute-start | bytes 7077896 | tf_op jit(solution)/shard_map/ppermute | solution.py:602
  449.4 112.7 %collective-permute-start.12 = (bf16[384,3072]{1,0:T(8,128)(2,1)}, bf16[384,3072]{1,0:T(8,128)(2,1)}, u32[]{:S(2)}, u32[]{:S(2)}) collective-permute-start(bf16[384,3072]{1,0:T(8,128)(2,1)} %add_convert_fusion.1), channel_id=1, source_target_pairs={{0,16},{16,0},{1,17},{17,1},{2,18},{18,2},{3,19},{19,3},{4,20},{20... | collective-permute-start | bytes 7077896 | tf_op jit(solution)/shard_map/ppermute | solution.py:602
  450.6 6.2 %collective-permute-start.9 = (bf16[16,384]{1,0:T(8,128)(2,1)S(1)}, bf16[16,384]{1,0:T(8,128)(2,1)S(1)}, u32[]{:S(2)}, u32[]{:S(2)}) collective-permute-start(bf16[16,384]{1,0:T(8,128)(2,1)S(1)} %dynamic-slice_convert_fusion.2), channel_id=1, source_target_pairs={{0,1},{1,0},{2,3},{3,2},{4,5},{5,4},{6,7},{7,6},{8,9},{9,8},{10,11... | collective-permute-start | bytes 36872 | tf_op jit(solution)/shard_map/ppermute | solution.py:602
  (16 other events, 71.0 us)
Sparse Core Ops, SparseCore 0:
  454.6 140.6 all-reduce.1

commit v2 on v1

v2 whole, which is shorter than its diff:
```python
from functools import partial

import jax
import jax.numpy as jnp
from jax import lax
from jax.experimental import pallas as pl
from jax.experimental.pallas import tpu as pltpu
from jax.sharding import PartitionSpec as P

HEADS = 12
EPSILON = 1e-06
F32 = jnp.float32
BF16 = jnp.bfloat16
VMEM = pl.BlockSpec(memory_space=pltpu.VMEM)
SMEM = pl.BlockSpec(memory_space=pltpu.SMEM)
ROUTER_ROW = 8


def mm(a, b):
    return lax.dot_general(a, b, (((1,), (0,)), ((), ())), preferred_element_type=F32)


def mm_nt(a, b):
    return lax.dot_general(a, b, (((1,), (1,)), ((), ())), preferred_element_type=F32)


def mm_tn(a, b):
    return lax.dot_general(a, b, (((0,), (0,)), ((), ())), preferred_element_type=F32)


def iota(shape, dim):
    return lax.broadcasted_iota(jnp.int32, shape, dim)


def row_of(column, size):
    return jnp.sum(jnp.where(iota((size, size), 0) == iota((size, size), 1), column, 0.0), axis=0, keepdims=True)


def column_of(row, size):
    return jnp.sum(jnp.where(iota((size, size), 0) == iota((size, size), 1), row, 0.0), axis=1, keepdims=True)


def normalise(values):
    centre = values - jnp.mean(values, axis=-1, keepdims=True)
    spread = jnp.mean(centre * centre, axis=-1, keepdims=True)
    scale = lax.rsqrt(spread + EPSILON)
    return centre * scale, scale


def norm_backward(grad, gain, xhat, scale):
    scaled = grad * gain
    along = jnp.mean(scaled * xhat, axis=-1, keepdims=True)
    return scale * (scaled - jnp.mean(scaled, axis=-1, keepdims=True) - xhat * along)


def assign_stage(routes, level, capacity, padded):
    rows = routes.shape[0]
    level_row = level.astype(F32)
    level_column = column_of(level_row, rows)
    me, other = iota((rows, rows), 0), iota((rows, rows), 1)
    ahead = (level_row > level_column) | ((level_row == level_column) & (other < me))
    lane = iota((rows, 128), 1)
    first, second = routes[:, 0:1], routes[:, 1:2]
    wants = jnp.where((lane == first) | (lane == second + 64), 1.0, 0.0)
    count = mm(jnp.where(ahead, 1.0, 0.0).astype(BF16), wants.astype(BF16))
    total = jnp.sum(wants, axis=0, keepdims=True)
    rank_one = jnp.sum(jnp.where(lane == first, count, 0.0), axis=1, keepdims=True)
    rank_two = jnp.sum(
        jnp.where(lane == second + 64, count, 0.0) + jnp.where(lane == second, total, 0.0),
        axis=1,
        keepdims=True,
    )
    slot_one = jnp.where(rank_one < capacity, first.astype(F32) * padded + rank_one, -1.0)
    slot_two = jnp.where(rank_two < capacity, second.astype(F32) * padded + rank_two, -1.0)
    return slot_one, slot_two


def batch_of(experts, padded):
    best = 1
    for count in range(1, experts + 1):
        if experts % count == 0 and count * padded <= 256 and (count * padded) % 16 == 0:
            best = count
    return best


def spread_stage(values, slot_one, slot_two, experts, padded, store, extra=None):
    rows, width = values.shape
    one, two = row_of(slot_one, rows).astype(jnp.int32), row_of(slot_two, rows).astype(jnp.int32)
    batch = batch_of(experts, padded)
    place = iota((batch * padded, rows), 0)
    for start in range(0, experts, batch):
        here = place + start * padded
        pick = jnp.where((here == one) | (here == two), 1.0, 0.0).astype(BF16)
        block = mm(pick, values).reshape(batch, padded, width)
        if extra is not None:
            parts = []
            for inner in range(batch):
                parts.append(extra(start + inner, block[inner]))
            block = jnp.stack(parts)
        store(start, batch, block.astype(BF16))


def with_rows(block, first_row, rows):
    place = iota(block.shape, 0)
    for step, row in enumerate(rows):
        wide = jnp.concatenate([row, jnp.zeros((1, block.shape[1] - row.shape[1]), F32)], axis=1)
        block = jnp.where(place == first_row + step, wide, block)
    return block


def pieces(value, count):
    parts = []
    for _ in range(count):
        part = value.astype(BF16).astype(F32)
        parts.append(part)
        value = value - part
    return parts


def bias_stage(lengths_ref, m, rows, store):
    own_start = lax.axis_index("seq") * rows
    span = lax.axis_size("seq") * rows
    ends = []
    total = 0
    for step in range(lengths_ref.shape[1]):
        total = total + lengths_ref[m, step]
        ends.append(total)

    def documents(place):
        found = jnp.zeros(place.shape, jnp.int32)
        for end in ends:
            found = found + jnp.where(place >= end, 1, 0)
        return found

    asked = documents(iota((1, rows), 1) + own_start)
    for half in range(2):
        start = own_start if half == 0 else span - rows - own_start
        held = documents(iota((rows, 1), 0) + start)
        store(half, jnp.where(held == asked, 0.0, -1e30))


def gates_of(logits, routes):
    lane = iota(logits.shape, 1)
    chosen = [
        jnp.sum(jnp.where(lane == routes[:, k : k + 1] + ROUTER_ROW, logits, 0.0), axis=1, keepdims=True)
        for k in range(2)
    ]
    peak = jnp.maximum(*chosen)
    raised = [jnp.exp(part - peak) for part in chosen]
    total = raised[0] + raised[1]
    return raised[0] / total, raised[1] / total


def phi_terms(hidden):
    size = jnp.abs(hidden)
    bell = jnp.exp(hidden * hidden * -0.5)
    t = 1.0 / (1.0 + 0.23164188828 * size)
    tail = t * (
        0.127414796
        + t * (-0.142248368 + t * (0.7107068705 + t * (-0.7265760135 + t * 0.5307027145)))
    )
    tail = tail * bell
    return jnp.where(hidden >= 0, 1.0 - tail, tail), bell


def gather_stage(blocks_ref, slots, weights, padded):
    experts, _, width = blocks_ref.shape
    rows = slots.shape[0]
    batch = batch_of(experts, padded)
    place = iota((rows, batch * padded), 1)
    totals = [jnp.zeros((rows, width), F32) for _ in weights]
    for start in range(0, experts, batch):
        block = (
            blocks_ref[start : start + batch].astype(F32).reshape(batch * padded, width).astype(BF16)
        )
        here = place + start * padded
        for index, chosen in enumerate(weights):
            hit = slots[:, chosen[0] : chosen[0] + 1] == here
            for k in chosen[1:]:
                hit = hit | (slots[:, k : k + 1] == here)
            totals[index] = totals[index] + mm(jnp.where(hit, 1.0, 0.0).astype(BF16), block)
    return totals


def mix_kernel(padded, back_ref, slots_ref, gates_ref, residual_ref, mixed_ref):
    gates = gates_ref[...]
    one, two = gather_stage(back_ref, slots_ref[...], ((0,), (1,)), padded)
    mixed_ref[...] = (
        residual_ref[...] + (gates[:, 0:1] * one + gates[:, 1:2] * two)
    ).astype(BF16)


MESH = pl.DeviceIdType.MESH
ANY = pl.BlockSpec(memory_space=pl.ANY)
CHUNK = 256


def remote(source, target, sends, arrives, device):
    return pltpu.make_async_remote_copy(
        src_ref=source,
        dst_ref=target,
        send_sem=sends,
        recv_sem=arrives,
        device_id=device,
        device_id_type=MESH,
    )


def greet(axes):
    barrier = pltpu.get_barrier_semaphore()
    count = 0
    for axis in axes:
        size, me = lax.axis_size(axis), lax.axis_index(axis)
        for step in range(1, size):
            pl.semaphore_signal(
                barrier, inc=1, device_id={axis: lax.rem(me + step, size)}, device_id_type=MESH
            )
            count += 1
    pl.semaphore_wait(barrier, count)


class Exchange:
    def __init__(self, source, target, sems, index):
        self.refs, self.index = (source, target, sems), index

    def copies(self):
        source, target, sems = self.refs
        size, me = lax.axis_size("exp"), lax.axis_index("exp")
        found = []
        for step in range(1, size):
            peer = lax.rem(me + step, size)
            found.append(
                remote(
                    source.at[peer],
                    target.at[me],
                    sems.at[self.index, 0, step],
                    sems.at[self.index, 1, step],
                    {"exp": peer},
                )
            )
        return found

    def own(self):
        source, target, sems = self.refs
        me = lax.axis_index("exp")
        return pltpu.make_async_copy(source.at[me], target.at[me], sems.at[self.index, 0, 0])

    def start(self):
        for copy in self.copies():
            copy.start()
        self.own().start()

    def arrived(self):
        for copy in self.copies():
            copy.wait_recv()
        self.own().wait()

    def sent(self):
        for copy in self.copies():
            copy.wait_send()


def project(low, weight_ref, parts, store):
    width = low.shape[1]
    for part in parts:
        block = mm(low, weight_ref[:, part * width : (part + 1) * width]).astype(BF16)
        for index in range(width // 128):
            store(part, index, block[:, index * 128 : (index + 1) * 128])


def attend_stage(query_ref, pair_ref, bias_ref, attended_ref, stats_ref):
    couples, rows, couple = query_ref.shape
    head_dim = couple // 2
    low_lane = iota((1, couple), 1) < head_dim

    def step(index, _):
        query = query_ref[index].astype(F32) * head_dim**-0.5
        keys = [pair_ref[half, 2 * index] for half in range(2)]
        values = [pair_ref[half, 2 * index + 1].astype(F32).T.astype(BF16) for half in range(2)]
        outs = []
        for head in range(2):
            mine = jnp.where(low_lane == (head == 0), query, 0.0).astype(BF16)
            scores = [mm_nt(keys[half], mine) + bias_ref[half] for half in range(2)]
            peak = jnp.maximum(*[jnp.max(part, axis=0, keepdims=True) for part in scores])
            raised = [jnp.exp(part - peak) for part in scores]
            total = sum(jnp.sum(part, axis=0, keepdims=True) for part in raised)
            here = slice(head * head_dim, (head + 1) * head_dim)
            summed = sum(mm(values[half][here], raised[half].astype(BF16)) for half in range(2))
            outs.append(summed / total)
            stats_ref[pl.ds(index * 2 + head, 1), :] = peak + jnp.log(total)
        lanes = pl.ds(pl.multiple_of(index * couple, couple), couple)
        attended_ref[:, lanes] = jnp.concatenate(outs, axis=0).T.astype(BF16)
        return 0

    lax.fori_loop(0, couples, step, 0)


def flatten_stage(rows_ref, cot_ref, x, g, capacity):
    experts, padded, width = rows_ref.shape
    batch = batch_of(experts, padded)
    flat = batch * padded
    place, lane = iota((padded, 128), 0), iota((padded, 128), 1)
    for start in range(0, experts, batch):
        block = rows_ref[start : start + batch].astype(F32)
        cot = cot_ref[start : start + batch].astype(F32)
        here = slice(start * padded, start * padded + flat)
        x[here, :] = block.reshape(flat, width).astype(BF16)
        scaled = []
        for inner in range(batch):
            inside = (place == capacity) | (place == capacity + 1)
            gate_row = jnp.sum(jnp.where(inside, block[inner][:, 0:128], 0.0), axis=0, keepdims=True)
            gate = jnp.sum(jnp.where(place == lane, gate_row, 0.0), axis=1, keepdims=True)
            scaled.append(cot[inner] * gate)
        g[here, :] = jnp.stack(scaled).reshape(flat, width).astype(BF16)


def expert_step(x, g, y, dx, up, down):
    hidden = mm(x[...], up)
    active_grad = mm_nt(g[...], down)
    phi, bell = phi_terms(hidden)
    active = (hidden * phi).astype(BF16)
    hidden_grad = (active_grad * (phi + hidden * bell * 0.3989422804)).astype(BF16)
    y[...] += mm(active, down)
    dx[...] += mm_nt(hidden_grad, up)
    return mm_tn(x[...], hidden_grad), mm_tn(active, g[...])


def finish_stage(cot_ref, y, dx, back_ref, grads_ref, capacity):
    experts, padded, width = cot_ref.shape
    batch = batch_of(experts, padded)
    place, lane = iota((padded, 128), 0), iota((padded, 128), 1)
    for start in range(0, experts, batch):
        here = slice(start * padded, (start + batch) * padded)
        produced = y[here, :].reshape(batch, padded, width).astype(BF16)
        back_ref[start : start + batch] = produced
        cot = cot_ref[start : start + batch].astype(F32)
        along = jnp.sum(cot * produced.astype(F32), axis=-1, keepdims=True)
        grads = dx[here, :].reshape(batch, padded, width)
        parts = []
        for inner in range(batch):
            row = jnp.sum(jnp.where(place == lane, along[inner], 0.0), axis=0, keepdims=True)
            parts.append(with_rows(grads[inner], capacity, pieces(row, 3)))
        grads_ref[start : start + batch] = jnp.stack(parts).astype(BF16)


def forward_kernel(
    capacity,
    tokens_ref,
    cot_ref,
    routes_ref,
    priority_ref,
    lengths_ref,
    pack_own,
    in_own,
    out_own,
    up_own,
    down_own,
    pack_out,
    in_out,
    out_out,
    token_out,
    query_out,
    pair_out,
    residual_out,
    moe_out,
    attended_out,
    stats_out,
    gates_out,
    slots_out,
    back_out,
    grads_out,
    up_old,
    down_old,
    up_keep,
    down_keep,
    up_got,
    down_got,
    up_sum,
    down_sum,
    up_arrived,
    pk,
    wi,
    wo,
    up,
    down,
    token_other,
    cot_send,
    row_send,
    cot_got,
    row_got,
    all_sems,
    weight_sems,
    token_sems,
    out_sems,
    chunk_sems,
    past_sems,
    low_sems,
    got_sems,
    cross_sems,
):
    micro_count, rows, width = tokens_ref.shape
    experts, padded = cot_send.shape[1], cot_send.shape[2]
    flat = experts * padded
    core, half_seq = lax.axis_index("dp"), lax.axis_index("seq")
    partner = {"dp": 1 - core}
    across = {"seq": 1 - half_seq}
    greet(("seq", "exp", "dp"))

    token_copies = [
        remote(
            tokens_ref.at[m], token_other.at[m], token_sems.at[m, 0], token_sems.at[m, 1], across
        )
        for m in range(micro_count)
    ]
    weights = []
    for index, (own, full) in enumerate(
        ((pack_own, pk), (in_own, wi), (out_own, wo), (up_own, up), (down_own, down))
    ):
        size = own.shape[0]
        place = full.at[core] if index == 0 else full.at[pl.ds(core * size, size)]
        weights.append(
            (
                remote(own, place, weight_sems.at[index, 0], weight_sems.at[index, 1], partner),
                pltpu.make_async_copy(own, place, weight_sems.at[index, 2]),
            )
        )
    token_copies[0].start()
    for index in range(3):
        weights[index][0].start()
        weights[index][1].start()
    token_copies[1].start()
    for index in range(3, 5):
        weights[index][0].start()
        weights[index][1].start()

    def have(index):
        weights[index][0].wait_recv()
        weights[index][1].wait()

    cots = [Exchange(cot_send.at[m], cot_got.at[m], all_sems, m) for m in range(micro_count)]
    rowses = [Exchange(row_send.at[m], row_got.at[m], all_sems, 2 + m) for m in range(micro_count)]
    gradses = [Exchange(cot_send.at[m], grads_out.at[m], all_sems, 4 + m) for m in range(micro_count)]
    lane_two = iota((rows, slots_out.shape[2]), 1)

    def claim(m):
        one, two = assign_stage(routes_ref[m], priority_ref[m], capacity, padded)
        slots_out[m] = jnp.where(lane_two == 0, one, two).astype(jnp.int32)

        def store(start, batch, block):
            cot_send[m, start : start + batch] = block

        spread_stage(cot_ref[m], one, two, experts, padded, store)

    used = [0]

    def keep(refs, later):
        index = used[0]
        used[0] += 1

        def copy():
            source, target = refs()
            return pltpu.make_async_copy(source, target, out_sems.at[index])

        copy().start()
        later.append(copy)

    late = []
    claim(0)
    cots[0].start()
    have(0)
    pack_out[...] = jnp.concatenate([pk[0], pk[1]], axis=1)

    def gain(row):
        return pack_out[row : row + 1].astype(F32)

    def first_norm(values):
        return (normalise(values.astype(F32))[0] * gain(0) + gain(1)).astype(BF16)

    def attention_phase(query, pair, bias, residual, moe, attended):
        def project_own(m):
            def store(part, index, block):
                if part == 0:
                    query[m, index] = block
                else:
                    pair[m, 0, 2 * index + part - 1] = block

            project(first_norm(tokens_ref[m]), wi, range(3), store)

        def project_other(m):
            def store(part, index, block):
                pair[m, 1, 2 * index + part - 1] = block

            project(first_norm(token_other[m]), wi, range(1, 3), store)

        have(1)
        for m in range(micro_count):
            project_own(m)
        claim(1)
        have(2)
        keep(lambda: (wi, in_out), late)
        keep(lambda: (wo, out_out), late)
        outs, local = [], []
        for m in range(micro_count):
            token_copies[m].wait_recv()
            project_other(m)
            keep(lambda m=m: (token_other.at[m], token_out.at[m]), late)
            keep(lambda m=m: (query.at[m], query_out.at[m]), outs)
            keep(lambda m=m: (pair.at[m], pair_out.at[m]), outs)

            def store_bias(half, block):
                bias[half] = block

            bias_stage(lengths_ref, m, rows, store_bias)
            for copy in local:
                copy().wait()
            attend_stage(query.at[m], pair.at[m], bias, attended, stats_out.at[m])
            summed = tokens_ref[m].astype(F32) + mm(attended[...], wo[...])
            residual[...] = summed
            moe_input = (normalise(summed)[0] * gain(2) + gain(3)).astype(BF16)
            moe[...] = moe_input
            gates = gates_of(mm_nt(moe_input, pack_out[...]), routes_ref[m])
            gates_out[m] = jnp.where(lane_two == 0, gates[0], gates[1])
            slots = slots_out[m]
            slot_cols = [slots[:, k : k + 1] for k in range(2)]
            place = iota((rows, 128), 1)

            def gate_rows(expert, block):
                row = sum(
                    jnp.where(slot_cols[k] - expert * padded == place, gates[k], 0.0)
                    for k in range(2)
                )
                return with_rows(block, capacity, pieces(jnp.sum(row, axis=0, keepdims=True), 2))

            def store(start, batch, block):
                row_send[m, start : start + batch] = block

            spread_stage(
                moe_input,
                slot_cols[0].astype(F32),
                slot_cols[1].astype(F32),
                experts,
                padded,
                store,
                gate_rows,
            )
            rowses[m].start()
            if m == 0:
                cots[1].start()
            local = []
            keep(lambda m=m: (residual, residual_out.at[m]), local)
            keep(lambda m=m: (moe, moe_out.at[m]), local)
            keep(lambda m=m: (attended, attended_out.at[m]), local)
        for copy in outs + local:
            copy().wait()

    pl.run_scoped(
        attention_phase,
        pltpu.VMEM((micro_count, width // 128, rows, 128), BF16),
        pltpu.VMEM((micro_count, 2, width // 64, rows, 128), BF16),
        pltpu.VMEM((2, rows, rows), F32),
        pltpu.VMEM((rows, width), F32),
        pltpu.VMEM((rows, width), BF16),
        pltpu.VMEM((rows, width), BF16),
    )
    have(3)
    have(4)
    chunks = up.shape[1] // CHUNK
    half_chunks = chunks // 2
    half_rows = width // 2

    def expert_phase(x, g, y, dx, up_buf, down_buf, up_past, down_past, up_low, down_low):
        def order(i):
            return lax.rem(i + core * half_chunks, chunks)

        def span(i):
            return pl.ds(pl.multiple_of(order(i) * CHUNK, CHUNK), CHUNK)

        def chunk_out(slot, i):
            return (
                pltpu.make_async_copy(up_buf.at[slot], up_old.at[i], chunk_sems.at[slot, 0]),
                pltpu.make_async_copy(down_buf.at[slot], down_old.at[i], chunk_sems.at[slot, 1]),
            )

        def chunk_past(slot, i):
            return (
                pltpu.make_async_copy(up_old.at[i], up_past.at[slot], past_sems.at[slot, 0]),
                pltpu.make_async_copy(down_old.at[i], down_past.at[slot], past_sems.at[slot, 1]),
            )

        def up_kept(slot, i):
            mine = up_buf.at[slot, pl.ds(core * half_rows, half_rows)]
            return pltpu.make_async_copy(mine, up_keep.at[order(i)], chunk_sems.at[slot, 0])

        def up_given(slot, i):
            place = order(i)
            return remote(
                up_low.at[slot], up_got.at[place], low_sems.at[slot, 0], got_sems.at[0, place], partner
            )

        def down_kept(slot, i):
            return pltpu.make_async_copy(
                down_buf.at[slot], down_keep.at[lax.rem(i, half_chunks)], chunk_sems.at[slot, 1]
            )

        def down_given(slot, i):
            place = lax.rem(i, half_chunks)
            return remote(
                down_low.at[slot],
                down_got.at[place],
                low_sems.at[slot, 1],
                got_sems.at[1, place],
                partner,
            )

        def start_expert(m):
            cots[m].arrived()
            rowses[m].arrived()
            flatten_stage(row_got.at[m], cot_got.at[m], x, g, capacity)
            y[...] = jnp.zeros_like(y)
            dx[...] = jnp.zeros_like(dx)

        def end_expert(m):
            cots[m].sent()
            rowses[m].sent()
            finish_stage(cot_got.at[m], y, dx, row_send.at[m], cot_send.at[m], capacity)
            gradses[m].start()
            keep(lambda m=m: (row_send.at[m], back_out.at[m]), late)

        start_expert(0)

        def first_pass(i, _):
            slot = lax.rem(i, 2)
            up_grad, down_grad = expert_step(x, g, y, dx, up[:, span(i)], down[span(i), :])

            @pl.when(i >= 2)
            def _():
                for copy in chunk_out(slot, i - 2):
                    copy.wait()

            up_buf[slot] = up_grad
            down_buf[slot] = down_grad
            for copy in chunk_out(slot, i):
                copy.start()
            return 0

        lax.fori_loop(0, chunks, first_pass, 0)
        end_expert(0)
        for i in range(chunks - 2, chunks):
            for copy in chunk_out(i % 2, i):
                copy.wait()
        for copy in chunk_past(0, 0):
            copy.start()
        start_expert(1)

        def second_pass(i, _):
            slot = lax.rem(i, 2)

            @pl.when(i + 1 < chunks)
            def _():
                for copy in chunk_past(1 - slot, i + 1):
                    copy.start()

            up_grad, down_grad = expert_step(x, g, y, dx, up[:, span(i)], down[span(i), :])
            for copy in chunk_past(slot, i):
                copy.wait()

            @pl.when(i >= 2)
            def _():
                up_kept(slot, i - 2).wait()
                up_given(slot, i - 2).wait_send()

                @pl.when(i - 2 < half_chunks)
                def _():
                    down_kept(slot, i - 2).wait()

                @pl.when(i - 2 >= half_chunks)
                def _():
                    down_given(slot, i - 2).wait_send()

            up_buf[slot] = up_grad + up_past[slot]
            up_kept(slot, i).start()
            up_low[slot] = up_buf[slot, pl.ds((1 - core) * half_rows, half_rows), :].astype(BF16)
            up_given(slot, i).start()

            @pl.when(i < half_chunks)
            def _():
                down_buf[slot] = down_grad + down_past[slot]
                down_kept(slot, i).start()

            @pl.when(i >= half_chunks)
            def _():
                down_low[slot] = (down_grad + down_past[slot]).astype(BF16)
                down_given(slot, i).start()

            return 0

        lax.fori_loop(0, chunks, second_pass, 0)
        end_expert(1)
        for i in range(chunks - 2, chunks):
            up_kept(i % 2, i).wait()
            up_given(i % 2, i).wait_send()
            down_given(i % 2, i).wait_send()

    pl.run_scoped(
        expert_phase,
        pltpu.VMEM((flat, width), BF16),
        pltpu.VMEM((flat, width), BF16),
        pltpu.VMEM((flat, width), F32),
        pltpu.VMEM((flat, width), F32),
        pltpu.VMEM((2, width, CHUNK), F32),
        pltpu.VMEM((2, CHUNK, width), F32),
        pltpu.VMEM((2, width, CHUNK), F32),
        pltpu.VMEM((2, CHUNK, width), F32),
        pltpu.VMEM((2, width // 2, CHUNK), BF16),
        pltpu.VMEM((2, CHUNK, width), BF16),
    )

    def sum_phase(up_mine, up_theirs, up_total, down_mine, down_theirs, down_total):
        def loads(kind, slot, i):
            mine, theirs, kept, got = (
                (up_mine, up_theirs, up_keep, up_got),
                (down_mine, down_theirs, down_keep, down_got),
            )[kind]
            return (
                pltpu.make_async_copy(kept.at[i], mine.at[slot], chunk_sems.at[slot, 0]),
                pltpu.make_async_copy(got.at[i], theirs.at[slot], chunk_sems.at[slot, 1]),
            )

        def stores(kind, slot, i):
            total, kept = ((up_total, up_sum), (down_total, down_sum))[kind]
            here = pl.ds(pl.multiple_of(i * CHUNK, CHUNK), CHUNK)
            target = kept.at[:, here] if kind == 0 else kept.at[here]
            return pltpu.make_async_copy(total.at[slot], target, past_sems.at[slot, kind])

        def taken(kind, i):
            low, got = ((up_total, up_got), (down_total, down_got))[kind]
            remote(
                low.at[0], got.at[i], low_sems.at[0, kind], got_sems.at[kind, i], partner
            ).wait_recv()

        for kind, count in ((0, chunks), (1, half_chunks)):
            mine, theirs, total = (
                (up_mine, up_theirs, up_total),
                (down_mine, down_theirs, down_total),
            )[kind]
            taken(kind, 0)
            for copy in loads(kind, 0, 0):
                copy.start()

            def step(i, _):
                slot = lax.rem(i, 2)

                @pl.when(i + 1 < count)
                def _():
                    taken(kind, i + 1)
                    for copy in loads(kind, 1 - slot, i + 1):
                        copy.start()

                for copy in loads(kind, slot, i):
                    copy.wait()

                @pl.when(i >= 2)
                def _():
                    stores(kind, slot, i - 2).wait()

                total[slot] = (mine[slot] + theirs[slot].astype(F32)).astype(BF16)
                stores(kind, slot, i).start()
                return 0

            lax.fori_loop(0, count, step, 0)
            for i in range(count - 2, count):
                stores(kind, i % 2, i).wait()
            if kind == 0:
                cross.start()

    cross = remote(up_sum, up_arrived, cross_sems.at[0], cross_sems.at[1], across)
    pl.run_scoped(
        sum_phase,
        pltpu.VMEM((2, half_rows, CHUNK), F32),
        pltpu.VMEM((2, half_rows, CHUNK), BF16),
        pltpu.VMEM((2, half_rows, CHUNK), BF16),
        pltpu.VMEM((2, CHUNK, width), F32),
        pltpu.VMEM((2, CHUNK, width), BF16),
        pltpu.VMEM((2, CHUNK, width), BF16),
    )
    for m in range(micro_count):
        token_copies[m].wait_send()
        gradses[m].arrived()
        gradses[m].sent()
    for index in range(5):
        weights[index][0].wait_send()
    for copy in late:
        copy().wait()
    cross.wait()


def back_stage(
    m,
    capacity,
    padded,
    grads_ref,
    slots,
    gates,
    routes,
    cot,
    residual,
    moe_input,
    attended_ref,
    stats_ref,
    query_ref,
    pair_ref,
    lengths_ref,
    pack,
    wo_ref,
    wi_ref,
    tokens,
    token_other,
    residual_grad_ref,
    out_grad_ref,
    in_grad_ref,
    first_grad_ref,
    other_grad_ref,
    small_ref,
    bias_ref,
    attended_grad_ref,
    packed_ref,
    add,
):
    rows, width = residual.shape
    couples, _, couple = query_ref.shape
    head_dim = couple // 2
    experts = grads_ref.shape[0]
    gain = [pack[row : row + 1].astype(F32) for row in range(4)]

    def store_bias(half, block):
        bias_ref[half] = block

    bias_stage(lengths_ref, m, rows, store_bias)
    (moe_grad,) = gather_stage(grads_ref, slots, ((0, 1),), padded)
    place, lane = iota((padded, 128), 0), iota((rows, 128), 1)
    found = [jnp.zeros((rows, 128), F32) for _ in range(2)]
    for expert in range(experts):
        tail = grads_ref[expert][:, 0:128].astype(F32)
        inside = (place >= capacity) & (place < capacity + 3)
        row = jnp.sum(jnp.where(inside, tail, 0.0), axis=0, keepdims=True)
        for k in range(2):
            found[k] = found[k] + jnp.where(
                slots[:, k : k + 1] - expert * padded == lane, row, 0.0
            )
    gate_grad = [jnp.sum(part, axis=1, keepdims=True) for part in found]
    gate = [gates[:, k : k + 1] for k in range(2)]
    inner = gate[0] * gate_grad[0] + gate[1] * gate_grad[1]
    pack_lane = iota((rows, pack.shape[0]), 1)
    logit_grad = sum(
        jnp.where(
            pack_lane == routes[:, k : k + 1] + ROUTER_ROW, gate[k] * (gate_grad[k] - inner), 0.0
        )
        for k in range(2)
    )
    parts = [part.astype(BF16) for part in pieces(logit_grad, 3)]
    moe_grad = moe_grad + sum(mm(part, pack) for part in parts)
    router_grad = sum(mm_tn(part, moe_input) for part in parts)
    xhat, scale = normalise(residual)
    small_row = iota(router_grad.shape, 0)
    small = jnp.where(
        small_row == 2,
        jnp.sum(moe_grad * xhat, axis=0, keepdims=True),
        jnp.where(small_row == 3, jnp.sum(moe_grad, axis=0, keepdims=True), router_grad),
    )
    small_ref[...] = small
    residual_grad = cot.astype(F32) + norm_backward(moe_grad, gain[2], xhat, scale)
    residual_grad_ref[...] = residual_grad
    branch = residual_grad.astype(BF16)
    add(out_grad_ref, slice(0, width), mm_tn(attended_ref[...], branch))
    attended_grad = mm_nt(branch, wo_ref[...]).astype(BF16)
    for index in range(couples):
        attended_grad_ref[index] = attended_grad[:, index * couple : (index + 1) * couple]
    low_lane = iota((1, couple), 1) < head_dim

    def step(index, _):
        query = query_ref[index].astype(F32) * head_dim**-0.5
        grad_low = attended_grad_ref[index]
        grad = grad_low.astype(F32)
        query_low = query.astype(BF16)
        keys = [pair_ref[half, 2 * index] for half in range(2)]
        values = [pair_ref[half, 2 * index + 1] for half in range(2)]
        keys_turned = [part.astype(F32).T.astype(BF16) for part in keys]
        key_grads, value_grads, query_grads = [[], []], [[], []], []
        for head in range(2):
            chosen = low_lane == (head == 0)
            mine = jnp.where(chosen, query, 0.0).astype(BF16)
            mine_grad = jnp.where(chosen, grad, 0.0).astype(BF16)
            stats = stats_ref[pl.ds(index * 2 + head, 1), :]
            weighting = [
                jnp.exp(mm_nt(keys[half], mine) + bias_ref[half] - stats) for half in range(2)
            ]
            weighting_grad = [mm_nt(values[half], mine_grad) for half in range(2)]
            delta = sum(
                jnp.sum(weighting[half] * weighting_grad[half], axis=0, keepdims=True)
                for half in range(2)
            )
            here = slice(head * head_dim, (head + 1) * head_dim)
            query_total = 0.0
            for half in range(2):
                scores_grad = (weighting[half] * (weighting_grad[half] - delta)).astype(BF16)
                value_grads[half].append(mm(weighting[half].astype(BF16), grad_low))
                key_grads[half].append(mm(scores_grad, query_low))
                query_total = query_total + mm(keys_turned[half][here], scores_grad)
            query_grads.append(query_total * head_dim**-0.5)

        def lanes(part):
            return pl.ds(pl.multiple_of(part * width + index * couple, couple), couple)

        packed_ref[0:rows, lanes(0)] = jnp.concatenate(query_grads, axis=0).T.astype(BF16)
        for half in range(2):
            here = slice(half * rows, (half + 1) * rows)
            packed_ref[here, lanes(1)] = jnp.where(low_lane, *key_grads[half]).astype(BF16)
            packed_ref[here, lanes(2)] = jnp.where(low_lane, *value_grads[half]).astype(BF16)
        return 0

    lax.fori_loop(0, couples, step, 0)
    own_xhat = normalise(tokens.astype(F32))[0]
    other_xhat = normalise(token_other.astype(F32))[0]
    low = jnp.concatenate([own_xhat, other_xhat], axis=0) * gain[0] + gain[1]
    low = low.astype(BF16)
    first_grad = mm_nt(packed_ref[0:rows, 0:width], wi_ref[:, 0:width])
    other_grad = 0.0
    add(in_grad_ref, slice(0, width), mm_tn(low[0:rows], packed_ref[0:rows, 0:width]))
    for part in range(1, 3):
        here = slice(part * width, (part + 1) * width)
        add(in_grad_ref, here, mm_tn(low, packed_ref[:, here]))
        first_grad = first_grad + mm_nt(packed_ref[0:rows, here], wi_ref[:, here])
        other_grad = other_grad + mm_nt(packed_ref[rows:, here], wi_ref[:, here])
    first_grad_ref[...] = first_grad
    other_grad_ref[...] = other_grad.astype(BF16)


def last_stage(tokens, gain, residual_grad, first_grad, arrived):
    xhat, scale = normalise(tokens.astype(F32))
    total = first_grad + arrived.astype(F32)
    return (
        (residual_grad + norm_backward(total, gain, xhat, scale)).astype(BF16),
        jnp.sum(total * xhat, axis=0, keepdims=True),
        jnp.sum(total, axis=0, keepdims=True),
    )


def put(ref, here, value):
    ref[:, here] = value


def back_kernel(
    m,
    capacity,
    padded,
    grads_ref,
    slots_ref,
    gates_ref,
    routes_ref,
    cot_ref,
    residual_ref,
    moe_ref,
    attended_ref,
    stats_ref,
    query_ref,
    pair_ref,
    lengths_ref,
    pack_ref,
    wo_ref,
    wi_ref,
    tokens_ref,
    token_other_ref,
    residual_grad_ref,
    out_grad_ref,
    in_grad_ref,
    first_grad_ref,
    other_grad_ref,
    small_ref,
    bias_ref,
    attended_grad_ref,
    packed_ref,
):
    back_stage(
        m,
        capacity,
        padded,
        grads_ref,
        slots_ref[...],
        gates_ref[...],
        routes_ref[...],
        cot_ref[...],
        residual_ref[...],
        moe_ref[...],
        attended_ref,
        stats_ref,
        query_ref,
        pair_ref,
        lengths_ref,
        pack_ref[...],
        wo_ref,
        wi_ref,
        tokens_ref[...],
        token_other_ref[...],
        residual_grad_ref,
        out_grad_ref,
        in_grad_ref,
        first_grad_ref,
        other_grad_ref,
        small_ref,
        bias_ref,
        attended_grad_ref,
        packed_ref,
        put,
    )


def last_kernel(
    tokens_ref, pack_ref, residual_grad_ref, first_grad_ref, arrived_ref, small_in, out_ref, small_ref
):
    grads, gain_grad, shift_grad = last_stage(
        tokens_ref[...],
        pack_ref[0:1].astype(F32),
        residual_grad_ref[...],
        first_grad_ref[...],
        arrived_ref[...],
    )
    out_ref[...] = grads
    row = iota(small_ref.shape, 0)
    small_ref[...] = jnp.where(row == 0, gain_grad, jnp.where(row == 1, shift_grad, small_in[...]))


def shape(dims, dtype):
    return jax.ShapeDtypeStruct(dims, dtype)


def call(kernel, outs, specs, scratch=(), name=None, flops=10**9):
    return pl.pallas_call(
        kernel,
        out_shape=outs,
        in_specs=specs,
        out_specs=tuple(VMEM for _ in outs),
        scratch_shapes=scratch,
        compiler_params=pltpu.CompilerParams(vmem_limit_bytes=56 * 2**20),
        cost_estimate=pl.CostEstimate(flops=flops, bytes_accessed=10**7, transcendentals=0),
        name=name,
    )


def body(
    tokens,
    first_gain,
    first_shift,
    attention_in,
    attention_out,
    second_gain,
    second_shift,
    router_weight,
    up_weight,
    down_weight,
    routes,
    priority,
    lengths,
    out_cotangent,
):
    micro_count, _, rows, width = tokens.shape
    experts = lax.axis_size("exp") * up_weight.shape[0]
    hidden = up_weight.shape[2]
    capacity = (210 * rows + 100 * experts - 1) // (100 * experts)
    padded = (capacity + 3 + 7) // 8 * 8
    flat = experts * padded
    core = lax.axis_index("dp")
    chunks = hidden // CHUNK
    couples = width // 128

    def swap(value, axis):
        return lax.ppermute(value, axis, [(0, 1), (1, 0)])

    pack_rows = (ROUTER_ROW + experts + 15) // 16 * 16
    norms = jnp.stack([first_gain, first_shift, second_gain, second_shift])
    pack = jnp.concatenate(
        [
            norms,
            jnp.zeros((ROUTER_ROW - 4, norms.shape[1]), BF16),
            router_weight.T,
            jnp.zeros((pack_rows - ROUTER_ROW - experts, norms.shape[1]), BF16),
        ]
    )
    blocks = (micro_count, experts, padded, width)
    token_dims = (micro_count, rows, width)
    dma = pltpu.SemaphoreType.DMA
    tokens, cot = tokens[:, 0], out_cotangent[:, 0]
    routes, lengths = routes[:, 0], lengths[:, 0]
    query_dims = (micro_count, couples, rows, 128)
    pair_dims = (micro_count, 2, 2 * couples, rows, 128)
    outs = (
        (VMEM, (pack_rows, width), BF16),
        (ANY, (width, 3 * width), BF16),
        (ANY, (width, width), BF16),
        (ANY, token_dims, BF16),
        (ANY, query_dims, BF16),
        (ANY, pair_dims, BF16),
        (ANY, token_dims, F32),
        (ANY, token_dims, BF16),
        (ANY, token_dims, BF16),
        (VMEM, (micro_count, 16, rows), F32),
        (VMEM, (micro_count, rows, 2), F32),
        (VMEM, (micro_count, rows, 2), jnp.int32),
        (ANY, blocks, BF16),
        (ANY, blocks, BF16),
        (ANY, (chunks, width, CHUNK), F32),
        (ANY, (chunks, CHUNK, width), F32),
        (ANY, (chunks, width // 2, CHUNK), F32),
        (ANY, (chunks // 2, CHUNK, width), F32),
        (ANY, (chunks, width // 2, CHUNK), BF16),
        (ANY, (chunks // 2, CHUNK, width), BF16),
        (ANY, (width // 2, hidden), BF16),
        (ANY, (hidden // 2, width), BF16),
        (ANY, (width // 2, hidden), BF16),
    )
    size = lax.axis_size("exp")
    (
        pack,
        wi,
        wo,
        token_other,
        query,
        pair,
        residual,
        moe,
        attended,
        stats,
        gates,
        slots,
        back,
        grads,
        _,
        _,
        _,
        _,
        _,
        _,
        up_sum,
        down_sum,
        up_arrived,
    ) = pl.pallas_call(
        partial(forward_kernel, capacity),
        out_shape=tuple(shape(dims, dtype) for _, dims, dtype in outs),
        in_specs=[VMEM] * 4 + [SMEM] + [ANY] * 5,
        out_specs=tuple(spec for spec, _, _ in outs),
        scratch_shapes=[
            pltpu.VMEM((2, pack_rows, width // 2), BF16),
            pltpu.VMEM((width, 3 * width), BF16),
            pltpu.VMEM((width, width), BF16),
            pltpu.VMEM((width, hidden), BF16),
            pltpu.VMEM((hidden, width), BF16),
            pltpu.VMEM(token_dims, BF16),
            pltpu.VMEM(blocks, BF16),
            pltpu.VMEM(blocks, BF16),
            pltpu.VMEM(blocks, BF16),
            pltpu.VMEM(blocks, BF16),
            dma((6, 2, size)),
            dma((5, 3)),
            dma((micro_count, 2)),
            dma((24,)),
            dma((2, 2)),
            dma((2, 2)),
            dma((2, 2)),
            dma((2, chunks)),
            dma((2,)),
        ],
        compiler_params=pltpu.CompilerParams(
            collective_id=0, has_side_effects=True, vmem_limit_bytes=61 * 2**20
        ),
        cost_estimate=pl.CostEstimate(
            flops=5 * 10**10, bytes_accessed=10**8, transcendentals=10**7
        ),
        name="forward_and_experts",
    )(tokens, cot, routes, priority, lengths, pack, attention_in, attention_out, up_weight[0], down_weight[0])
    arrived = [
        lax.all_to_all(back[m], "exp", split_axis=0, concat_axis=0, tiled=True)
        for m in range(micro_count)
    ]
    mixed_parts, token_grads = [], []
    in_sum = out_sum = small_sum = 0.0
    for m in range(micro_count):
        residual_grad, out_grad, in_grad, first_grad, other_grad, small = call(
            partial(back_kernel, m, capacity, padded),
            (
                shape((rows, width), F32),
                shape((width, width), F32),
                shape((width, 3 * width), F32),
                shape((rows, width), F32),
                shape((rows, width), BF16),
                shape((pack_rows, width), F32),
            ),
            [VMEM] * 11 + [SMEM] + [VMEM] * 5,
            (
                pltpu.VMEM((2, rows, rows), F32),
                pltpu.VMEM((couples, rows, 128), BF16),
                pltpu.VMEM((2 * rows, 3 * width), BF16),
            ),
            name="attend_back",
        )(
            grads[m],
            slots[m],
            gates[m],
            routes[m],
            cot[m],
            residual[m],
            moe[m],
            attended[m],
            stats[m],
            query[m],
            pair[m],
            lengths,
            pack,
            wo,
            wi,
            tokens[m],
            token_other[m],
        )
        tokens_grad, small = call(
            last_kernel,
            (shape((rows, width), BF16), shape((pack_rows, width), F32)),
            [VMEM] * 6,
            name="tokens_back",
        )(tokens[m], pack, residual_grad, first_grad, swap(other_grad, "seq"), small)
        (mixed,) = call(
            partial(mix_kernel, padded), (shape((rows, width), BF16),), [VMEM] * 4, name="mix"
        )(arrived[m], slots[m], gates[m], residual[m])
        mixed_parts.append(mixed)
        token_grads.append(tokens_grad)
        in_sum = in_sum + in_grad
        out_sum = out_sum + out_grad
        small_sum = small_sum + small

    def halves(value, axis):
        size = value.shape[axis] // 2
        mine = lax.dynamic_slice_in_dim(value, core * size, size, axis)
        theirs = lax.dynamic_slice_in_dim(value, (1 - core) * size, size, axis)
        return mine + swap(theirs.astype(BF16), "dp").astype(F32)

    up_total = (up_sum.astype(F32) + up_arrived.astype(F32))[None]
    down_total = (down_sum.astype(F32) + swap(down_sum, "seq").astype(F32))[None]
    dense = halves(jnp.concatenate([in_sum, out_sum], axis=1), 0).astype(BF16)
    dense = lax.psum(dense, ("seq", "exp")).astype(F32)
    small = halves(small_sum, 1)
    small = lax.psum(small, ("seq", "exp"))
    return (
        jnp.stack(mixed_parts)[:, None],
        jnp.stack(token_grads)[:, None],
        small[0],
        small[1],
        dense[:, : 3 * width],
        dense[:, 3 * width :],
        small[2],
        small[3],
        small[ROUTER_ROW : ROUTER_ROW + experts].T,
        up_total,
        down_total,
    )


def solution(mesh):
    placed = (
        P(None, ("exp", "dp"), "seq", None),
        P("dp"),
        P("dp"),
        P("dp", None),
        P("dp", None),
        P("dp"),
        P("dp"),
        P("dp", None),
        P("exp", "dp", None),
        P("exp", "dp", None),
        P(None, ("exp", "dp"), "seq", None),
        P(None, ("exp", "dp"), "seq"),
        P(None, ("exp", "dp"), None),
        P(None, ("exp", "dp"), "seq", None),
    )
    return jax.shard_map(
        body,
        mesh=mesh,
        in_specs=placed,
        out_specs=(
            P(None, ("exp", "dp"), "seq", None),
            P(None, ("exp", "dp"), "seq", None),
            P("dp"),
            P("dp"),
            P("dp", None),
            P("dp", None),
            P("dp"),
            P("dp"),
            P("dp", None),
            P("exp", "dp", None),
            P("exp", "dp", None),
        ),
        check_vma=False,
    )
```

time: 616 us -> 576 us (0.935)
  Pallas kernels: 218 us -> 320 us
  waiting for transfers between devices: 118 us -> 56.3 us
  starting transfers between devices: 57 us -> 19.6 us
  blocking collectives: 112 us -> 86.5 us
  other arithmetic: 56.3 us -> 31.8 us
    pallas_call x12 -> x5, Pallas kernels: 210 us -> 311 us  [the longest x1 240 us: body(): pl.pallas_call(partial(forward_kernel, capacity), out_shape=tuple((shape(...]
    ppermute x15 -> x5, waiting for transfers between devices: 64 us -> 0.01 us  [swap(): return lax.ppermute(value, axis, [(0, 1), (1, 0)])]
    all_to_all x1 -> x0, blocking collectives: 34.1 us -> none  [exchange(): return lax.all_to_all(value, 'exp', split_axis=0, concat_axis=0, tiled=True)]
    all_to_all x7 -> x2, starting transfers between devices: 48.4 us -> 17.3 us  [body(): lax.all_to_all(back[m], 'exp', split_axis=0, concat_axis=0, tiled=True)]
    select_n x5 -> x0, other arithmetic: 19.8 us -> none  [whole(): jnp.where(core == 0, jnp.concatenate([value, got], axis=axis), jnp.concat...]
    squeeze x4 -> x11, local copies, waits for them, and re-layouts: 5.77 us -> 19 us  [the longest x1 3.33 us: body(): residual[m]]
    convert_element_type x2 -> x0, other arithmetic: 10.5 us -> none  [pair_sum(): low = value.astype(BF16)]
    convert_element_type x3 -> x1, local copies, waits for them, and re-layouts: 8.29 us -> 0.01 us  [halves(): return mine + swap(theirs.astype(BF16), 'dp').astype(F32)]
  transfers between devices with their start and end apart: 23 -> 8, of which waited for: 7 -> 2; matrix products, arithmetic and copies ran while one was open for 12% -> 4% of each run, Pallas kernels for 35% -> 3%
where the time goes in v2:
time: 576 us; the launch traced here: 566 us
  Pallas kernels  320 us (56%)
  blocking collectives  86.5 us (15%)
  waiting for transfers between devices  56.3 us (10%)
  local copies, waits for them, and re-layouts  37.1 us (6%)
  other arithmetic  31.8 us (6%)
  starting transfers between devices  19.6 us (3%)
  between operations  14.6 us (3%)
    pallas_call x1, Pallas kernels, body(): pl.pallas_call(partial(forward_kernel, capacity), out_shape=tuple((shape(...  240 us
    psum x1, blocking collectives, body(): small = lax.psum(small, ('seq', 'exp'))  86.5 us
    pallas_call x2, Pallas kernels, body(): call(partial(back_kernel, m, capacity, padded), (shape((rows, width), F32...  63.7 us
    all_to_all x2, waiting for transfers between devices, body(): lax.all_to_all(back[m], 'exp', split_axis=0, concat_axis=0, tiled=True)  29.3 us
    psum x1, waiting for transfers between devices, body(): dense = lax.psum(dense, ('seq', 'exp')).astype(F32)  27 us
    all_to_all x2, starting transfers between devices, body(): lax.all_to_all(back[m], 'exp', split_axis=0, concat_axis=0, tiled=True)  17.3 us
  transfers between devices with their start and end apart: 8, of which 2 were waited for; matrix products, arithmetic and copies ran while one was open for 4% of the time, Pallas kernels for 3%

profile of v2, /device:TPU:0, one launch (start us, length us, event | category | flops | bytes accessed | tf_op | source)
XLA Modules:
  0.0 565.5 jit_solution(8459972248534876642)
XLA Ops:
  7.2 1.6 copy.25
  12.2 3.1 slice_bitcast_fusion.18
  16.5 239.5 %forward_and_experts.1 = (bf16[16,768]{1,0:T(8,128)(2,1)}, bf16[768,2304]{1,0:T(8,128)(2,1)}, bf16[768,768]{1,0:T(8,128)(2,1)}, bf16[2,384,768]{2,1,0:T(8,128)(2...) custom-call(bf16[2,384,768]{2,1,0:T(8,128)(2,1)} %bitcast.79, ...), custom_call_target="tpu_custom_call" | custom-call | flops 49999998976 | bytes 100000000 | tf_op jit(solution)/shard_map/forward_and_experts/pallas_call | solution.py:1145
  256.1 3.3 slice_bitcast_fusion.7
  259.4 1.8 slice_bitcast_fusion.22
  262.0 2.5 slice_bitcast_fusion.1
  264.9 1.6 slice_bitcast_fusion.3
  271.6 1.5 slice_bitcast_fusion.14
  273.1 31.7 %attend_back.2 = (f32[384,768]{1,0:T(8,128)}, f32[768,768]{1,0:T(8,128)}, f32[768,2304]{1,0:T(8,128)}, f32[384,768]{1,0:T(8,128)}, bf16[384,768]{1,0:T(8,128)(2,1)}, /*index=5*/f32[16,768]{1,0:T(8,128)}) custom-call(bf16[8,104,768]{2,1,0:T(8,128)(2,1)} %get-tuple-element.94.grads_ref, s32[384,2]{1,0:T(8,128)} %get-tuple-element.114.slots_ref, ...), custom_call_target="tpu_custom_call" | custom-call | flops 1000000000 | bytes 10000000 | tf_op jit(solution)/shard_map/attend_back/pallas_call | solution.py:1186
  304.8 31.9 %attend_back.3 = (f32[384,768]{1,0:T(8,128)}, f32[768,768]{1,0:T(8,128)}, f32[768,2304]{1,0:T(8,128)}, f32[384,768]{1,0:T(8,128)}, bf16[384,768]{1,0:T(8,128)(2,1)}, /*index=5*/f32[16,768]{1,0:T(8,128)}) custom-call(bf16[8,104,768]{2,1,0:T(8,128)(2,1)} %get-tuple-element.95.grads_ref, s32[384,2]{1,0:T(8,128)} %get-tuple-element.115.slots_ref, ...), custom_call_target="tpu_custom_call" | custom-call | flops 1000000000 | bytes 10000000 | tf_op jit(solution)/shard_map/attend_back/pallas_call | solution.py:1186
  336.7 2.1 add.38
  338.9 1.6 copy-done.1
  340.5 6.7 %add.37 = f32[768,2304]{1,0:T(8,128)} add(f32[768,2304]{1,0:T(8,128)S(1)} %copy-done.1, f32[768,2304]{1,0:T(8,128)} %get-tuple-element.71) | non-fusion elementwise | flops 1769472 | bytes 21233664 | tf_op jit(solution)/shard_map/add | solution.py:1233
  347.2 3.9 fusion.1
  351.1 1.6 slice_bitcast_fusion.5
  352.7 13.1 %all-to-all-start = ((bf16[8,104,768]{2,1,0:T(8,128)(2,1)}), bf16[8,104,768]{2,1,0:T(8,128)(2,1)}, u32[]{:S(2)}, u32[]{:S(2)}) async-start(bf16[8,104,768]{2,1,0:T(8,128)(2,1)} %get-tuple-element.96), calls=%async_computation | async-start | bytes 2555904 | tf_op jit(solution)/shard_map/all_to_all | solution.py:1180
  365.9 2.0 collective-permute-start.1
  368.0 29.3 %all-to-all-done.back_ref = bf16[8,104,768]{2,1,0:T(8,128)(2,1)} async-done(((bf16[8,104,768]{2,1,0:T(8,128)(2,1)}), bf16[8,104,768]{2,1,0:T(8,128)(2,1)}, u32[]{:S(2)}, u32[]{:S(2)}) %all-to-all-start) | async-done | bytes 1277984 | tf_op jit(solution)/shard_map/all_to_all | solution.py:1180
  397.3 4.3 all-to-all-start.1
  401.6 4.8 fusion.4
  406.5 1.6 copy-done.7
  408.1 4.7 add_bitcast_fusion.1
  412.8 4.1 tokens_back.2
  416.9 3.8 tokens_back.3
  421.6 2.2 maximum_bitcast_fusion.1
  423.8 86.5 %psum.14 = f32[16,384]{1,0:T(8,128)S(1)} all-reduce(f32[16,384]{1,0:T(8,128)S(1)} %convert_add_fusion), channel_id=1, replica_groups=mesh['seq'=2,'exp'=8,'dp'=2] {'seq','exp'}, use_global_device_ids=true, to_apply=%region_0.0 | all-reduce | flops 6144 | bytes 49152 | tf_op jit(solution)/shard_map/psum | solution.py:1248
  511.5 4.2 mix.2
  515.8 4.2 mix.3
  520.0 2.2 maximum_bitcast_fusion
  522.2 4.3 add_bitcast_fusion
  526.5 27.0 %all-reduce.2.cloned.1.call-done = bf16[384,3072]{1,0:T(8,128)(2,1)} async-done(((bf16[384,3072]{1,0:T(8,128)(2,1)}), bf16[384,3072]{1,0:T(8,128)(2,1)}) %all-reduce.2.cloned.1.call-update) | async-done | bytes 2359312 | tf_op jit(solution)/shard_map/psum | solution.py:1246
  553.5 3.6 slice.156
  (69 shorter events, 14.3 us)
Async XLA Ops:
  12.2 3.1 copy-start.17
  256.1 5.1 copy-start.14
  256.1 5.9 %copy-start.2 = (bf16[2,2,12,384,128]{4,3,2,1,0:T(8,128)(2,1)S(1)}, bf16[2,2,12,384,128]{4,3,2,1,0:T(8,128)(2,1)}, u32[]{:S(2)}) copy-start(bf16[2,2,12,384,128]{4,3,2,1,0:T(8,128)(2,1)} %get-tuple-element.54) | copy-start | bytes 14155780
  262.0 2.8 copy-start.4
  264.9 1.7 copy-start.9
  266.5 1.7 copy-start.8
  266.6 2.7 copy-start.15
  266.6 5.0 copy-start.10
  266.6 5.0 copy-start.11
  304.8 31.9 %copy-start.5 = (f32[768,768]{1,0:T(8,128)S(1)}, f32[768,768]{1,0:T(8,128)}, u32[]{:S(2)}) copy-start(f32[768,768]{1,0:T(8,128)} %get-tuple-element.72) | copy-start | bytes 7077892
  336.7 3.7 copy-start.1
  347.2 3.9 copy-start.3
  351.1 50.5 %collective-permute-start.3 = (bf16[384,3072]{1,0:T(8,128)(2,1)}, bf16[384,3072]{1,0:T(8,128)(2,1)}, u32[]{:S(2)}, u32[]{:S(2)}) collective-permute-start(bf16[384,3072]{1,0:T(8,128)(2,1)} %fusion.1), channel_id=1, source_target_pairs={{0,1},{1,0},{2,3},{3,2},{4,5},{5,4},{6,7},{7,6},{8,9},{9,8},{10,11... | collective-permute-start | bytes 7077896 | tf_op jit(solution)/shard_map/ppermute | solution.py:1076
  352.7 13.1 %copy-start.18 = (bf16[384,768]{1,0:T(8,128)(2,1)S(1)}, bf16[384,768]{1,0:T(8,128)(2,1)}, u32[]{:S(2)}) copy-start(bf16[384,768]{1,0:T(8,128)(2,1)} %get-tuple-element.60) | copy-start | bytes 1769476
  352.7 13.2 %copy-start.19 = (bf16[384,768]{1,0:T(8,128)(2,1)S(1)}, bf16[384,768]{1,0:T(8,128)(2,1)}, u32[]{:S(2)}) copy-start(bf16[384,768]{1,0:T(8,128)(2,1)} %get-tuple-element.65) | copy-start | bytes 1769476
  352.7 44.5 %all-to-all-start = ((bf16[8,104,768]{2,1,0:T(8,128)(2,1)}), bf16[8,104,768]{2,1,0:T(8,128)(2,1)}, u32[]{:S(2)}, u32[]{:S(2)}) async-start(bf16[8,104,768]{2,1,0:T(8,128)(2,1)} %get-tuple-element.96), calls=%async_computation | async-start | bytes 2555904 | tf_op jit(solution)/shard_map/all_to_all | solution.py:1180
  365.8 47.0 %collective-permute-start = (bf16[384,768]{1,0:T(8,128)(2,1)S(1)}, bf16[384,768]{1,0:T(8,128)(2,1)}, u32[]{:S(2)}, u32[]{:S(2)}) collective-permute-start(bf16[384,768]{1,0:T(8,128)(2,1)S(1)} %copy-done.18), channel_id=1, source_target_pairs={{0,16},{16,0},{1,17},{17,1},{2,18},{18,2},{3,19},{19,3},{4,20},{20... | collective-permute-start | bytes 1769480 | tf_op jit(solution)/shard_map/ppermute | solution.py:1076
  365.9 51.0 %collective-permute-start.1 = (bf16[384,768]{1,0:T(8,128)(2,1)S(1)}, bf16[384,768]{1,0:T(8,128)(2,1)}, u32[]{:S(2)}, u32[]{:S(2)}) collective-permute-start(bf16[384,768]{1,0:T(8,128)(2,1)S(1)} %copy-done.19), channel_id=1, source_target_pairs={{0,16},{16,0},{1,17},{17,1},{2,18},{18,2},{3,19},{19,3},{4,20},{20... | collective-permute-start | bytes 1769480 | tf_op jit(solution)/shard_map/ppermute | solution.py:1076
  367.9 154.3 %collective-permute-start.4 = (bf16[1536,768]{1,0:T(8,128)(2,1)}, bf16[1536,768]{1,0:T(8,128)(2,1)}, u32[]{:S(2)}, u32[]{:S(2)}) collective-permute-start(bf16[1536,768]{1,0:T(8,128)(2,1)} %get-tuple-element.76), channel_id=1, source_target_pairs={{0,16},{16,0},{1,17},{17,1},{2,18},{18,2},{3,19},{19,3},{4,20},{20... | collective-permute-start | bytes 7077896 | tf_op jit(solution)/shard_map/ppermute | solution.py:1076
  397.3 118.5 %all-to-all-start.1 = ((bf16[8,104,768]{2,1,0:T(8,128)(2,1)}), bf16[8,104,768]{2,1,0:T(8,128)(2,1)}, u32[]{:S(2)}, u32[]{:S(2)}) async-start(bf16[8,104,768]{2,1,0:T(8,128)(2,1)} %get-tuple-element.97), calls=%async_computation.1 | async-start | bytes 2555904 | tf_op jit(solution)/shard_map/all_to_all | solution.py:1180
  401.6 152.0 %all-reduce.2.cloned.1.call-start = ((), (), s32[]{:S(2)}) async-start(), calls=%async_computation.2 | async-start | bytes 4718592 | tf_op jit(solution)/shard_map/psum | solution.py:1246
  406.4 1.7 copy-start.7
  416.9 3.8 copy-start.16
  416.9 4.7 copy-start.12
  421.5 2.3 collective-permute-start.2
  515.7 4.3 copy-start.13
  515.7 6.5 %copy-start.6 = (bf16[1536,768]{1,0:T(8,128)(2,1)S(1)}, bf16[1536,768]{1,0:T(8,128)(2,1)}, u32[]{:S(2)}) copy-start(bf16[1536,768]{1,0:T(8,128)(2,1)} %get-tuple-element.76) | copy-start | bytes 7077892
  553.5 3.7 copy-start
Sparse Core Ops, SparseCore 0:
  408.6 144.8 all-reduce.1
